TPU v7x, 256 devices: a whole 4x4x8 slice. The times are simulated.
256 devices in a mesh: recv: 64 (over y, x, z_hi), seg: 4 (over z_lo, core).
Axes of the slice: x: 4, y: 4, z: 8 (z_hi: 4, z_lo: 2; z = z_hi * 2 + z_lo), core: 2. Of those that a mesh axis runs over, the one named last changes fastest.
Arguments:
- raw_data: float32 [8, 4096, 2048], P('seg', 'recv'), may hold values from -210 to 210
- row_owner: int32 [4096, 1], P('recv'), may hold values from 0 to 63; in each aligned block of 64 rows (0 to 63, 64 to 127, ...) at most 2 rows name the same one
- source_blocks: int32 [2], replicated, may hold values from 0 to 63, as said below
Outputs:
- correlations: bfloat16 [2, 128, 8192, 512], P(None, 'seg', 'recv')
Inputs may be any that keep to these rules, and one draw needn't show every extreme that they name: `row_owner`: within the rows of one device (aligned blocks of 64 rows) no owner is named by more than 2 rows, a bound that some block reaches. `source_blocks`: the ids are distinct, and one of them is always the last block; block b covers channel slots b * 128 to (b + 1) * 128 - 1.
All inputs are finite; a program needn't handle non-finite values. Where the computation divides by a largest or mean magnitude, that divisor is 1e-20 or more.
Results may differ from a plain program's by a relative error of at most 0.0068.
Values may be sent and summed in bfloat16 or wider, within the bound.
A program may use at most 128 MiB of HBM per device.

v0:
```python
import functools
import math

import jax
import jax.numpy as jnp
import numpy as np
from jax import lax
from jax.experimental import pallas as pl
from jax.experimental.pallas import tpu as pltpu
from jax.sharding import PartitionSpec as P

WIN = 512
NB = 128
HALF = 256


def forward_table():
    sample, freq = np.arange(WIN), np.arange(HALF)
    angles = (sample[:, None] * freq[None, :] % WIN) * (2.0 * math.pi / WIN)
    parity = np.where(sample % 2 == 0, 1.0, -1.0)
    sines = np.where(freq[None, :] == 0, parity[:, None], -np.sin(angles))
    return np.concatenate([np.cos(angles), sines], axis=1)


def inverse_table(window_total):
    lag, freq = np.arange(WIN) - HALF, np.arange(HALF)
    angles = (freq[:, None] * lag[None, :] % WIN) * (2.0 * math.pi / WIN)
    factor = 1.0 / (WIN * math.sqrt(window_total * WIN))
    parity = np.where(lag % 2 == 0, 1.0, -1.0)
    zero = freq[:, None] == 0
    cosine_rows = np.where(zero, factor, 2.0 * factor * np.cos(angles))
    sine_rows = np.where(zero, factor * parity[None, :], -2.0 * factor * np.sin(angles))
    return np.concatenate([cosine_rows, sine_rows], axis=0)


def prepare_kernel(blocks, raw, owner_column, owner_row, slots, chunk, flat):
    row = lax.broadcasted_iota(jnp.int32, (64, 512), 0)
    lane = lax.broadcasted_iota(jnp.int32, (64, 512), 1)
    same = (owner_column[...] == owner_row[...]) & (row < lane % 64)
    rank = jnp.sum(same.astype(jnp.int32), axis=0, keepdims=True)
    target = (owner_row[...] * 2 + rank) * 8 + lax.broadcasted_iota(jnp.int32, (1, 512), 1) // 64
    for n in range(2):
        for run in range(16):
            values = raw[n, :, run * NB : (run + 1) * NB]
            amplitude = jnp.mean(jnp.abs(values), axis=-1, keepdims=True) + 1e-06
            place = n * 4 + run // 4
            flat[place * 64 : place * 64 + 64, run % 4 * NB : run % 4 * NB + NB] = (
                values / amplitude
            ).astype(jnp.bfloat16)

    @pl.loop(0, 4)
    def _(part):
        placed = lax.broadcasted_iota(jnp.int32, (256, 512), 0) + part * 256 == target
        slots[pl.ds(pl.multiple_of(part * 256, 256), 256), :] = jnp.dot(
            placed.astype(jnp.float32).astype(jnp.bfloat16), flat[...], preferred_element_type=jnp.float32
        ).astype(jnp.bfloat16)

    for b in range(2):
        chunk[b * 16 : b * 16 + 16, :] = slots[pl.ds(pl.multiple_of(blocks[b] * 16, 16), 16), :]


def prepare(raw_data, row_owner, source_blocks):
    vmem = pl.BlockSpec(memory_space=pltpu.VMEM)
    return pl.pallas_call(
        prepare_kernel,
        out_shape=(
            jax.ShapeDtypeStruct((1024, WIN), jnp.bfloat16),
            jax.ShapeDtypeStruct((32, WIN), jnp.bfloat16),
        ),
        in_specs=[pl.BlockSpec(memory_space=pltpu.SMEM), vmem, vmem, vmem],
        out_specs=(vmem, vmem),
        scratch_shapes=[pltpu.VMEM((512, WIN), jnp.bfloat16)],
        compiler_params=pltpu.CompilerParams(vmem_limit_bytes=24 * 1024 * 1024),
        name="prepare",
    )(source_blocks, raw_data, row_owner, jnp.tile(row_owner.reshape(1, 64), (1, 8)))


MESH = pl.DeviceIdType.MESH
ORDER = (2, 1, 3, 0)


def exchange_kernel(slots, first, held, panels, staged, chunk, turn_send, turn_recv, xy_send, xy_recv, z_send, z_recv,
                    core_send, core_recv, pz_send, pz_recv, pxy_send, pxy_recv, local_sem):
    recv = lax.axis_index("recv")
    seg = lax.axis_index("seg")
    y, x, zh = recv // 16, (recv // 4) % 4, recv % 4
    zl, core = seg // 2, seg % 2
    plane = y * 4 + x

    def plane_peer(step):
        return ((y + step // 4) % 4) * 4 + (x + step % 4) % 4

    def xy_copy(turn, step):
        target = plane_peer(step)
        block = (zh + turn) % 4
        return pltpu.make_async_remote_copy(
            src_ref=slots.at[target, block],
            dst_ref=staged.at[block, plane],
            send_sem=xy_send.at[turn, step],
            recv_sem=xy_recv.at[turn, step],
            device_id=(target * 4 + zh, seg),
            device_id_type=MESH,
        )

    def z_copy(turn, low):
        block = (zh + turn) % 4
        return pltpu.make_async_remote_copy(
            src_ref=staged.at[block],
            dst_ref=held.at[seg, :, zh],
            send_sem=z_send.at[turn, low],
            recv_sem=z_recv.at[turn, zl],
            device_id=(plane * 4 + block, low * 2 + core),
            device_id_type=MESH,
        )

    def z_arrival(turn, low):
        place = (zh + 4 - turn) % 4
        return pltpu.make_async_remote_copy(
            src_ref=staged.at[0],
            dst_ref=held.at[low * 2 + core, :, place],
            send_sem=z_send.at[turn, low],
            recv_sem=z_recv.at[turn, low],
            device_id=(recv, seg),
            device_id_type=MESH,
        )

    def core_copy(turn, low):
        place = (zh + 4 - turn) % 4
        return pltpu.make_async_remote_copy(
            src_ref=held.at[low * 2 + core, :, place],
            dst_ref=held.at[low * 2 + core, :, place],
            send_sem=core_send.at[turn, low],
            recv_sem=core_recv.at[turn, low],
            device_id=(recv, zl * 2 + 1 - core),
            device_id_type=MESH,
        )

    def pz_copy(turn):
        return pltpu.make_async_remote_copy(
            src_ref=chunk,
            dst_ref=panels.at[plane, zh],
            send_sem=pz_send.at[turn],
            recv_sem=pz_recv.at[turn],
            device_id=(plane * 4 + (zh + turn) % 4, seg),
            device_id_type=MESH,
        )

    def pxy_copy(step):
        return pltpu.make_async_remote_copy(
            src_ref=panels.at[plane],
            dst_ref=panels.at[plane],
            send_sem=pxy_send.at[step],
            recv_sem=pxy_recv.at[step],
            device_id=(plane_peer(step) * 4 + zh, seg),
            device_id_type=MESH,
        )

    def turn_copy():
        return pltpu.make_async_remote_copy(
            src_ref=first,
            dst_ref=chunk,
            send_sem=turn_send,
            recv_sem=turn_recv,
            device_id=((seg * 4 + x) * 4 + zh, y),
            device_id_type=MESH,
        )

    barrier = pltpu.get_barrier_semaphore()

    @pl.when(y != seg)
    def _():
        pl.semaphore_signal(barrier, inc=1, device_id=((seg * 4 + x) * 4 + zh, y), device_id_type=MESH)

    @pl.loop(1, 16)
    def _(step):
        pl.semaphore_signal(barrier, inc=1, device_id=(plane_peer(step) * 4 + zh, seg), device_id_type=MESH)

    @pl.loop(1, 8)
    def _(step):
        z = (zh * 2 + zl + step) % 8
        pl.semaphore_signal(
            barrier, inc=1, device_id=(plane * 4 + z // 2, (z % 2) * 2 + core), device_id_type=MESH
        )

    pl.semaphore_signal(barrier, inc=1, device_id=(recv, zl * 2 + 1 - core), device_id_type=MESH)
    kept_chunk = pltpu.make_async_copy(first, chunk, local_sem.at[6])
    own_chunk = pltpu.make_async_copy(chunk, panels.at[plane, zh], local_sem.at[4])

    @pl.when(y == seg)
    def _():
        kept_chunk.start()

    own = []
    for turn in ORDER:
        block = (zh + turn) % 4
        own.append(pltpu.make_async_copy(slots.at[plane, block], staged.at[block, plane], local_sem.at[turn]))
        own[-1].start()
    @pl.when(y == seg)
    def _():
        pl.semaphore_wait(barrier, 23)

    @pl.when(y != seg)
    def _():
        pl.semaphore_wait(barrier, 24)
        turn_copy().start()

    for turn in ORDER[:1]:
        @pl.loop(1, 16)
        def _(step):
            xy_copy(turn, step).start()
    for turn in ORDER[1:]:
        @pl.loop(1, 16)
        def _(step):
            xy_copy(turn, step).start()

    @pl.when(y != seg)
    def _():
        turn_copy().wait()

    @pl.when(y == seg)
    def _():
        kept_chunk.wait()

    own_chunk.start()
    for turn in (1, 2, 3):
        pz_copy(turn).start()

    kept = None
    for number, turn in enumerate(ORDER):
        own[number].wait()

        @pl.loop(1, 16)
        def _(step):
            xy_copy(turn, step).wait_recv()

        if turn:
            z_copy(turn, 0).start()
            z_copy(turn, 1).start()
        else:
            z_copy(0, 1 - zl).start()
            kept = pltpu.make_async_copy(
                staged.at[zh], held.at[seg, :, zh], local_sem.at[5]
            )
            kept.start()
        if number == 0:
            own_chunk.wait()
            for other in (1, 2, 3):
                pz_copy(other).wait_recv()

            @pl.loop(1, 16)
            def _(step):
                pxy_copy(step).start()

    kept.wait()
    core_copy(0, zl).start()
    for turn in (1, 3, 2):
        for low in (0, 1):
            z_arrival(turn, low).wait_recv()
            core_copy(turn, low).start()
    z_arrival(0, 1 - zl).wait_recv()
    core_copy(0, 1 - zl).start()

    @pl.loop(1, 16)
    def _(step):
        pxy_copy(step).wait_recv()
        pxy_copy(step).wait_send()
        for turn in ORDER:
            xy_copy(turn, step).wait_send()

    for turn in (1, 2, 3):
        pz_copy(turn).wait_send()
        for low in (0, 1):
            z_copy(turn, low).wait_send()
    z_copy(0, 1 - zl).wait_send()
    for turn in range(4):
        for low in (0, 1):
            core_copy(turn, low).wait()


def exchange(slots, chunk):
    dma = pltpu.SemaphoreType.DMA
    rows, width = slots.shape[-2:]
    return pl.pallas_call(
        exchange_kernel,
        out_shape=(
            jax.ShapeDtypeStruct((4, 16, 4, rows, width), jnp.bfloat16),
            jax.ShapeDtypeStruct((16, 4) + chunk.shape, jnp.bfloat16),
        ),
        in_specs=[pl.BlockSpec(memory_space=pltpu.VMEM)] * 2,
        out_specs=(pl.BlockSpec(memory_space=pltpu.VMEM),) * 2,
        scratch_shapes=[
            pltpu.VMEM((4, 16, rows, width), jnp.bfloat16),
            pltpu.VMEM(chunk.shape, jnp.bfloat16),
            dma, dma, dma((4, 16)), dma((4, 16)), dma((4, 2)), dma((4, 2)), dma((4, 2)), dma((4, 2)),
            dma((4,)), dma((4,)), dma((16,)), dma((16,)), dma((7,)),
        ],
        compiler_params=pltpu.CompilerParams(
            collective_id=0, has_side_effects=True, vmem_limit_bytes=32 * 1024 * 1024
        ),
        name="exchange",
    )(slots, chunk)


NT=(((1,),(1,)),((),())); TN=(((0,),(0,)),((),()))
def body(held, panels, fwd, inv, out, x, rf, lt, ss, *, per):
    f32=jnp.float32; bf=jnp.bfloat16
    @pl.when(pl.program_id(0)==0)
    def _():
        row=lax.broadcasted_iota(jnp.int32,(256,256),0); col=lax.broadcasted_iota(jnp.int32,(256,256),1)
        perm=((row%32)//2*16+row%2*8+row//32==col).astype(f32).astype(bf)
        @pl.loop(0,16)
        def _(n):
            k=n//4; g=n%4
            y=jnp.dot(perm, held[k,pl.ds(g*16,16)].reshape(256,512), preferred_element_type=f32).astype(bf)
            for w in range(8):
                x[pl.ds(pl.multiple_of((k*8+w)*128+g*32,32),32),:]=y[w*32:(w+1)*32]
        @pl.loop(0,16)
        def _(n):
            v=lax.dot_general(fwd[...], x[pl.ds(pl.multiple_of(n*256,256),256),:], NT, preferred_element_type=f32)
            for dw in range(2):
                for c in range(2):
                    rf[pl.ds(c*32+n*2+dw,256,stride=72),:]=v[c*256:(c+1)*256,dw*128:(dw+1)*128]
        perm2=((row%16)//2*32+(row%32)//16*16+row%2*8+row//32==col).astype(f32).astype(bf)
        @pl.loop(0,8)
        def _(n):
            k=n//2; g=n%2
            y=jnp.dot(perm2, panels[pl.ds(n*8,8)].reshape(256,512), preferred_element_type=f32).astype(bf)
            for w in range(8):
                for b in range(2):
                    for h in range(2):
                        x[pl.ds(pl.multiple_of((k*8+w)*128+h*64+b*32+g*16,16),16),:]=y[w*32+b*16:w*32+b*16+16]
        lane=lax.broadcasted_iota(jnp.int32,(256,128),1)<64
        first=lax.broadcasted_iota(jnp.int32,(256,128),0)==0
        @pl.loop(0,16)
        def _(n):
            v=lax.dot_general(fwd[...], x[pl.ds(pl.multiple_of(n*256,256),256),:], NT, preferred_element_type=f32)
            for dw in range(2):
                re=v[:256,dw*128:(dw+1)*128]; im=v[256:,dw*128:(dw+1)*128]
                lt[pl.ds(n*2+dw,256,stride=72),:]=jnp.where(lane,re,jnp.where(first,0.0,-im))
                lt[pl.ds(32+n*2+dw,256,stride=72),:]=jnp.where(lane,jnp.where(first,0.0,im),jnp.where(first,im,re))
        @pl.loop(0,256,unroll=8)
        def _(j):
            at=pl.ds(pl.multiple_of(j*72,8),64)
            s=lax.dot_general(lt[at,:].astype(bf), rf[at,:].astype(bf), TN, preferred_element_type=f32)
            ss[pl.ds(j,64,stride=520),:]=s[:64]
            ss[pl.ds(256+j,64,stride=520),:]=s[64:]
    base=pl.program_id(0)*per
    @pl.loop(0,per,unroll=4)
    def _(i):
        v=ss[pl.ds(pl.multiple_of((base+i)*520,8),512),:].astype(bf)
        out[i]=lax.dot_general(v, inv[...], TN, preferred_element_type=f32).astype(bf)

def compute(held, panels, fwd, inv, per=8):
    one=pl.Buffered(1)
    def whole(a): return pl.BlockSpec(a.shape, lambda i: (0,)*a.ndim, pipeline_mode=one)
    return pl.pallas_call(functools.partial(body,per=per), grid=(64//per,),
        out_shape=jax.ShapeDtypeStruct((64,128,512),jnp.bfloat16),
        in_specs=[whole(held),whole(panels),whole(fwd),whole(inv)],
        out_specs=pl.BlockSpec((per,128,512),lambda i:(i,0,0)),
        scratch_shapes=[pltpu.VMEM((4096,512),jnp.bfloat16),pltpu.VMEM((256*72,128),jnp.float32),
            pltpu.VMEM((256*72,128),jnp.float32),pltpu.VMEM((64*520,128),jnp.float32)],
        compiler_params=pltpu.CompilerParams(vmem_limit_bytes=56*1024*1024), name="correlate")(held,panels,fwd,inv)


def local(raw_data, row_owner, source_blocks):
    slots, chunk = prepare(raw_data, row_owner, source_blocks)
    held, panels = exchange(slots.reshape(16, 4, 16, WIN), chunk)
    forward = jnp.asarray(forward_table().T, jnp.bfloat16)
    inverse = jnp.asarray(inverse_table(32), jnp.bfloat16)
    lagged = compute(
        held.reshape(4, 64, 16, WIN), panels.reshape(64, 32, WIN), forward, inverse
    )
    return lagged.reshape(2, 32, 128, WIN)


def solution(mesh):
    placed = (P("seg", "recv", None), P("recv", None), P())
    return jax.shard_map(
        local, mesh=mesh, in_specs=placed, out_specs=P(None, "seg", "recv", None), check_vma=False
    )
```

profile of v0, /device:TPU:1, one launch (start us, length us, event | category | flops | bytes accessed | tf_op | source)
XLA Modules:
  0.0 112.9 jit_solution(17028815932501666656)
XLA Ops:
  0.0 0.7 tile.11
  0.7 0.1 tile.12.owner_row
  0.7 0.7 copy.6.owner_column
  1.5 0.0 copy-start.2
  1.5 1.2 %copy-done.2 = f32[2,64,2048]{2,1,0:T(8,128)S(1)} copy-done((f32[2,64,2048]{2,1,0:T(8,128)S(1)}, f32[2,64,2048]{2,1,0:T(8,128)}, u32[]{:S(2)}) %copy-start.2) | copy-done | bytes 1048600
  2.7 0.0 copy-start.3
  2.7 0.7 copy-done.3
  3.4 2.1 %prepare.1 = (bf16[1024,512]{1,0:T(8,128)(2,1)S(1)}, bf16[32,512]{1,0:T(8,128)(2,1)S(1)}) custom-call(s32[2]{0:T(128)S(1)} %copy-done.3, f32[2,64,2048]{2,1,0:T(8,128)S(1)} %copy-done.2, s32[64,1]{1,0:T(8,128)S(1)} %copy.6.owner_column, s32[1,512]{1,0:T(1,128)S(1)} %tile.12.owner_row), custom_call_target="tpu_custom_call" | custom-call | tf_op jit(solution)/shard_map/prepare/pallas_call | solution.py:64
  5.5 67.0 %exchange.1 = (bf16[4,16,4,16,512]{4,3,2,1,0:T(8,128)(2,1)S(1)}, bf16[16,4,32,512]{3,2,1,0:T(8,128)(2,1)S(1)}) custom-call(bf16[16,4,16,512]{3,2,1,0:T(8,128)(2,1)S(1)} %bitcast.7, bf16[32,512]{1,0:T(8,128)(2,1)S(1)} %get-tuple-element.10.first), custom_call_target="tpu_custom_call" | custom-call | tf_op jit(solution)/shard_map/exchange/pallas_call | solution.py:283
  72.5 0.0 copy-start
  72.5 1.9 %copy-done = bf16[4,16,4,16,512]{4,3,2,1,0:T(8,128)(2,1)} copy-done((bf16[4,16,4,16,512]{4,3,2,1,0:T(8,128)(2,1)}, bf16[4,16,4,16,512]{4,3,2,1,0:T(8,128)(2,1)S(1)}, u32[]{:S(2)}) %copy-start) | copy-done | bytes 4194328
  74.5 0.0 copy-start.1
  74.5 1.3 %copy-done.1 = bf16[16,4,32,512]{3,2,1,0:T(8,128)(2,1)} copy-done((bf16[16,4,32,512]{3,2,1,0:T(8,128)(2,1)}, bf16[16,4,32,512]{3,2,1,0:T(8,128)(2,1)S(1)}, u32[]{:S(2)}) %copy-start.1) | copy-done | bytes 2097176
  75.8 37.1 %correlate.1 = bf16[64,128,512]{2,1,0:T(8,128)(2,1)} custom-call(bf16[4,64,16,512]{3,2,1,0:T(8,128)(2,1)} %bitcast.5, bf16[64,32,512]{2,1,0:T(8,128)(2,1)} %bitcast.6, bf16[512,512]{1,0:T(8,128)(2,1)} %constant.4.clone.fwd, bf16[512,512]{1,0:T(8,128)(2,1)} %constant.5.clone.inv), custom_call_target="tpu_custom_call" | custom-call | tf_op jit(solution)/shard_map/correlate/pallas_call | solution.py:356
Async XLA Ops:
  1.5 1.2 %copy-start.2 = (f32[2,64,2048]{2,1,0:T(8,128)S(1)}, f32[2,64,2048]{2,1,0:T(8,128)}, u32[]{:S(2)}) copy-start(f32[2,64,2048]{2,1,0:T(8,128)} %raw.1) | copy-start | bytes 3145732
  2.7 0.7 copy-start.3
  72.5 1.9 %copy-start = (bf16[4,16,4,16,512]{4,3,2,1,0:T(8,128)(2,1)}, bf16[4,16,4,16,512]{4,3,2,1,0:T(8,128)(2,1)S(1)}, u32[]{:S(2)}) copy-start(bf16[4,16,4,16,512]{4,3,2,1,0:T(8,128)(2,1)S(1)} %get-tuple-element.11) | copy-start | bytes 12582916
  74.5 1.3 %copy-start.1 = (bf16[16,4,32,512]{3,2,1,0:T(8,128)(2,1)}, bf16[16,4,32,512]{3,2,1,0:T(8,128)(2,1)S(1)}, u32[]{:S(2)}) copy-start(bf16[16,4,32,512]{3,2,1,0:T(8,128)(2,1)S(1)} %get-tuple-element.12) | copy-start | bytes 6291460
where the time goes:
time: 114 us; the launch traced here: 113 us
  Pallas kernels  106 us (93%)
  local copies, waits for them, and re-layouts  6.6 us (6%)
    pallas_call x1, Pallas kernels, exchange(): pl.pallas_call(exchange_kernel, out_shape=(jax.ShapeDtypeStruct((4, 16, 4...  67 us
    pallas_call x1, Pallas kernels, compute(): pl.pallas_call(functools.partial(body, per=per), grid=(64 // per,), out_s...  37.1 us
    unnamed x9, local copies, waits for them, and re-layouts  5.87 us

commit v1 on v0

--- a/solution.py
+++ b/solution.py
@@ -33,26 +33,36 @@
     return np.concatenate([cosine_rows, sine_rows], axis=0)
 
 
-def prepare_kernel(blocks, raw, owner_column, owner_row, slots, chunk, flat):
+def prepare_kernel(blocks, raw, owner, table, slots, chunk, spectra):
     row = lax.broadcasted_iota(jnp.int32, (64, 512), 0)
     lane = lax.broadcasted_iota(jnp.int32, (64, 512), 1)
-    same = (owner_column[...] == owner_row[...]) & (row < lane % 64)
+    diagonal = row[:, :64] == lane[:, :64]
+    owner_column = jnp.sum(jnp.where(diagonal, owner[...], 0), axis=1, keepdims=True)
+    owner_row = jnp.sum(jnp.where(row == lane % 64, owner_column, 0), axis=0, keepdims=True)
+    same = (owner_column == owner_row) & (row < lane % 64)
     rank = jnp.sum(same.astype(jnp.int32), axis=0, keepdims=True)
-    target = (owner_row[...] * 2 + rank) * 8 + lax.broadcasted_iota(jnp.int32, (1, 512), 1) // 64
-    for n in range(2):
-        for run in range(16):
-            values = raw[n, :, run * NB : (run + 1) * NB]
+    target = (owner_row * 2 + rank) * 8 + lax.broadcasted_iota(jnp.int32, (1, 512), 1) // 64
+    for window in range(8):
+        parts = []
+        for run in range(4):
+            start = (window % 4 * 4 + run) * NB
+            values = raw[window // 4, :, start : start + NB]
             amplitude = jnp.mean(jnp.abs(values), axis=-1, keepdims=True) + 1e-06
-            place = n * 4 + run // 4
-            flat[place * 64 : place * 64 + 64, run % 4 * NB : run % 4 * NB + NB] = (
-                values / amplitude
-            ).astype(jnp.bfloat16)
+            parts.append(values / amplitude)
+        spectra[window * 64 : window * 64 + 64, :] = jnp.dot(
+            jnp.concatenate(parts, axis=1),
+            table[...],
+            precision=lax.Precision.HIGHEST,
+            preferred_element_type=jnp.float32,
+        ).astype(jnp.bfloat16)
 
     @pl.loop(0, 4)
     def _(part):
         placed = lax.broadcasted_iota(jnp.int32, (256, 512), 0) + part * 256 == target
         slots[pl.ds(pl.multiple_of(part * 256, 256), 256), :] = jnp.dot(
-            placed.astype(jnp.float32).astype(jnp.bfloat16), flat[...], preferred_element_type=jnp.float32
+            placed.astype(jnp.float32).astype(jnp.bfloat16),
+            spectra[...],
+            preferred_element_type=jnp.float32,
         ).astype(jnp.bfloat16)
 
     for b in range(2):
@@ -72,14 +82,14 @@
         scratch_shapes=[pltpu.VMEM((512, WIN), jnp.bfloat16)],
         compiler_params=pltpu.CompilerParams(vmem_limit_bytes=24 * 1024 * 1024),
         name="prepare",
-    )(source_blocks, raw_data, row_owner, jnp.tile(row_owner.reshape(1, 64), (1, 8)))
+    )(source_blocks, raw_data, row_owner.reshape(1, 64), jnp.asarray(forward_table(), jnp.float32))
 
 
 MESH = pl.DeviceIdType.MESH
 ORDER = (2, 1, 3, 0)
 
 
-def exchange_kernel(slots, first, held, panels, staged, chunk, turn_send, turn_recv, xy_send, xy_recv, z_send, z_recv,
+def exchange_kernel(slots, first, held, panels, staged, chunk, turn_send, turn_recv, xy_send, xy_recv, z_send, z_recv, pair_send, pair_recv,
                     core_send, core_recv, pz_send, pz_recv, pxy_send, pxy_recv, local_sem):
     recv = lax.axis_index("recv")
     seg = lax.axis_index("seg")
@@ -102,25 +112,37 @@
             device_id_type=MESH,
         )
 
+    near = (None, 0, 1 - zl, 1)
+
     def z_copy(turn, low):
         block = (zh + turn) % 4
         return pltpu.make_async_remote_copy(
             src_ref=staged.at[block],
             dst_ref=held.at[seg, :, zh],
-            send_sem=z_send.at[turn, low],
+            send_sem=z_send.at[turn],
             recv_sem=z_recv.at[turn, zl],
             device_id=(plane * 4 + block, low * 2 + core),
             device_id_type=MESH,
         )
 
     def z_arrival(turn, low):
-        place = (zh + 4 - turn) % 4
         return pltpu.make_async_remote_copy(
             src_ref=staged.at[0],
-            dst_ref=held.at[low * 2 + core, :, place],
-            send_sem=z_send.at[turn, low],
+            dst_ref=held.at[low * 2 + core, :, (zh + 4 - turn) % 4],
+            send_sem=z_send.at[turn],
             recv_sem=z_recv.at[turn, low],
             device_id=(recv, seg),
+            device_id_type=MESH,
+        )
+
+    def pair_copy(turn, low):
+        place = held.at[low * 2 + core, :, (zh + 4 - turn) % 4]
+        return pltpu.make_async_remote_copy(
+            src_ref=place,
+            dst_ref=place,
+            send_sem=pair_send.at[turn, low],
+            recv_sem=pair_recv.at[turn, low],
+            device_id=(recv, (1 - zl) * 2 + core),
             device_id_type=MESH,
         )
 
@@ -234,8 +256,7 @@
             xy_copy(turn, step).wait_recv()
 
         if turn:
-            z_copy(turn, 0).start()
-            z_copy(turn, 1).start()
+            z_copy(turn, near[turn]).start()
         else:
             z_copy(0, 1 - zl).start()
             kept = pltpu.make_async_copy(
@@ -253,12 +274,16 @@
 
     kept.wait()
     core_copy(0, zl).start()
-    for turn in (1, 3, 2):
-        for low in (0, 1):
-            z_arrival(turn, low).wait_recv()
-            core_copy(turn, low).start()
+    direct, far = 1 + 2 * zl, 3 - 2 * zl
+    for turn, low in ((2, 1 - zl), (direct, 0), (direct, 1)):
+        z_arrival(turn, low).wait_recv()
+        pair_copy(turn, low).start()
+        core_copy(turn, low).start()
     z_arrival(0, 1 - zl).wait_recv()
     core_copy(0, 1 - zl).start()
+    for turn, low in ((2, zl), (far, 0), (far, 1)):
+        pair_copy(turn, low).wait_recv()
+        core_copy(turn, low).start()
 
     @pl.loop(1, 16)
     def _(step):
@@ -269,9 +294,10 @@
 
     for turn in (1, 2, 3):
         pz_copy(turn).wait_send()
-        for low in (0, 1):
-            z_copy(turn, low).wait_send()
+        z_copy(turn, near[turn]).wait_send()
     z_copy(0, 1 - zl).wait_send()
+    for turn, low in ((2, 1 - zl), (direct, 0), (direct, 1)):
+        pair_copy(turn, low).wait_send()
     for turn in range(4):
         for low in (0, 1):
             core_copy(turn, low).wait()
@@ -291,7 +317,8 @@
         scratch_shapes=[
             pltpu.VMEM((4, 16, rows, width), jnp.bfloat16),
             pltpu.VMEM(chunk.shape, jnp.bfloat16),
-            dma, dma, dma((4, 16)), dma((4, 16)), dma((4, 2)), dma((4, 2)), dma((4, 2)), dma((4, 2)),
+            dma, dma, dma((4, 16)), dma((4, 16)), dma((4,)), dma((4, 2)), dma((4, 2)), dma((4, 2)),
+            dma((4, 2)), dma((4, 2)),
             dma((4,)), dma((4,)), dma((16,)), dma((16,)), dma((7,)),
         ],
         compiler_params=pltpu.CompilerParams(
@@ -302,26 +329,29 @@
 
 
 NT=(((1,),(1,)),((),())); TN=(((0,),(0,)),((),()))
-def body(held, panels, fwd, inv, out, x, rf, lt, ss, *, per):
+def body(held, panels, inv, out, x, rf, lt, ss, *, per):
     f32=jnp.float32; bf=jnp.bfloat16
     @pl.when(pl.program_id(0)==0)
     def _():
         row=lax.broadcasted_iota(jnp.int32,(256,256),0); col=lax.broadcasted_iota(jnp.int32,(256,256),1)
+        eye=(row==col).astype(f32).astype(bf)
+        def turned(n,c):
+            return lax.dot_general(eye, x[pl.ds(pl.multiple_of(n*256,256),256),c*256:(c+1)*256], NT, preferred_element_type=f32)
         perm=((row%32)//2*16+row%2*8+row//32==col).astype(f32).astype(bf)
-        @pl.loop(0,16)
+        @pl.loop(0,16,unroll=2)
         def _(n):
             k=n//4; g=n%4
             y=jnp.dot(perm, held[k,pl.ds(g*16,16)].reshape(256,512), preferred_element_type=f32).astype(bf)
             for w in range(8):
                 x[pl.ds(pl.multiple_of((k*8+w)*128+g*32,32),32),:]=y[w*32:(w+1)*32]
-        @pl.loop(0,16)
+        @pl.loop(0,16,unroll=2)
         def _(n):
-            v=lax.dot_general(fwd[...], x[pl.ds(pl.multiple_of(n*256,256),256),:], NT, preferred_element_type=f32)
-            for dw in range(2):
-                for c in range(2):
-                    rf[pl.ds(c*32+n*2+dw,256,stride=72),:]=v[c*256:(c+1)*256,dw*128:(dw+1)*128]
+            for c in range(2):
+                v=turned(n,c)
+                for dw in range(2):
+                    rf[pl.ds(c*32+n*2+dw,256,stride=72),:]=v[:,dw*128:(dw+1)*128]
         perm2=((row%16)//2*32+(row%32)//16*16+row%2*8+row//32==col).astype(f32).astype(bf)
-        @pl.loop(0,8)
+        @pl.loop(0,8,unroll=2)
         def _(n):
             k=n//2; g=n%2
             y=jnp.dot(perm2, panels[pl.ds(n*8,8)].reshape(256,512), preferred_element_type=f32).astype(bf)
@@ -331,11 +361,11 @@
                         x[pl.ds(pl.multiple_of((k*8+w)*128+h*64+b*32+g*16,16),16),:]=y[w*32+b*16:w*32+b*16+16]
         lane=lax.broadcasted_iota(jnp.int32,(256,128),1)<64
         first=lax.broadcasted_iota(jnp.int32,(256,128),0)==0
-        @pl.loop(0,16)
+        @pl.loop(0,16,unroll=2)
         def _(n):
-            v=lax.dot_general(fwd[...], x[pl.ds(pl.multiple_of(n*256,256),256),:], NT, preferred_element_type=f32)
+            real, imag = turned(n,0), turned(n,1)
             for dw in range(2):
-                re=v[:256,dw*128:(dw+1)*128]; im=v[256:,dw*128:(dw+1)*128]
+                re=real[:,dw*128:(dw+1)*128]; im=imag[:,dw*128:(dw+1)*128]
                 lt[pl.ds(n*2+dw,256,stride=72),:]=jnp.where(lane,re,jnp.where(first,0.0,-im))
                 lt[pl.ds(32+n*2+dw,256,stride=72),:]=jnp.where(lane,jnp.where(first,0.0,im),jnp.where(first,im,re))
         @pl.loop(0,256,unroll=8)
@@ -350,25 +380,24 @@
         v=ss[pl.ds(pl.multiple_of((base+i)*520,8),512),:].astype(bf)
         out[i]=lax.dot_general(v, inv[...], TN, preferred_element_type=f32).astype(bf)
 
-def compute(held, panels, fwd, inv, per=8):
+def compute(held, panels, inv, per=8):
     one=pl.Buffered(1)
     def whole(a): return pl.BlockSpec(a.shape, lambda i: (0,)*a.ndim, pipeline_mode=one)
     return pl.pallas_call(functools.partial(body,per=per), grid=(64//per,),
         out_shape=jax.ShapeDtypeStruct((64,128,512),jnp.bfloat16),
-        in_specs=[whole(held),whole(panels),whole(fwd),whole(inv)],
+        in_specs=[whole(held),whole(panels),whole(inv)],
         out_specs=pl.BlockSpec((per,128,512),lambda i:(i,0,0)),
         scratch_shapes=[pltpu.VMEM((4096,512),jnp.bfloat16),pltpu.VMEM((256*72,128),jnp.float32),
             pltpu.VMEM((256*72,128),jnp.float32),pltpu.VMEM((64*520,128),jnp.float32)],
-        compiler_params=pltpu.CompilerParams(vmem_limit_bytes=56*1024*1024), name="correlate")(held,panels,fwd,inv)
+        compiler_params=pltpu.CompilerParams(vmem_limit_bytes=56*1024*1024), name="correlate")(held,panels,inv)
 
 
 def local(raw_data, row_owner, source_blocks):
     slots, chunk = prepare(raw_data, row_owner, source_blocks)
     held, panels = exchange(slots.reshape(16, 4, 16, WIN), chunk)
-    forward = jnp.asarray(forward_table().T, jnp.bfloat16)
     inverse = jnp.asarray(inverse_table(32), jnp.bfloat16)
     lagged = compute(
-        held.reshape(4, 64, 16, WIN), panels.reshape(64, 32, WIN), forward, inverse
+        held.reshape(4, 64, 16, WIN), panels.reshape(64, 32, WIN), inverse
     )
     return lagged.reshape(2, 32, 128, WIN)
 

time: 114 us -> 103 us (0.904); the launches traced: 113 us -> 103 us
  Pallas kernels: 106 us -> 96.3 us
    pallas_call x1, Pallas kernels: 67 us -> 58.9 us  [exchange(): pl.pallas_call(exchange_kernel, out_shape=(jax.ShapeDtypeStruct((4, 16, 4...]
    pallas_call x1, Pallas kernels: 37.1 us -> 30.6 us  [compute(): pl.pallas_call(functools.partial(body, per=per), grid=(64 // per,), out_s...]
    pallas_call x1, Pallas kernels: 2.13 us -> 6.74 us  [prepare(): pl.pallas_call(prepare_kernel, out_shape=(jax.ShapeDtypeStruct((1024, WIN...]
    unnamed x9 -> x12, local copies, waits for them, and re-layouts: 5.87 us -> 7.02 us
where the time goes in v1:
time: 103 us
  Pallas kernels  96.3 us (93%)
  local copies, waits for them, and re-layouts  7.02 us (7%)
    pallas_call x1, Pallas kernels, exchange(): pl.pallas_call(exchange_kernel, out_shape=(jax.ShapeDtypeStruct((4, 16, 4...  58.9 us
    pallas_call x1, Pallas kernels, compute(): pl.pallas_call(functools.partial(body, per=per), grid=(64 // per,), out_s...  30.6 us
    unnamed x12, local copies, waits for them, and re-layouts  7.02 us
    pallas_call x1, Pallas kernels, prepare(): pl.pallas_call(prepare_kernel, out_shape=(jax.ShapeDtypeStruct((1024, WIN...  6.74 us

profile of v1, /device:TPU:1, one launch (start us, length us, event | category | flops | bytes accessed | tf_op | source)
XLA Modules:
  0.0 103.3 jit_solution(7359274560965529668)
XLA Ops:
  0.0 0.0 copy-start.2
  0.0 1.2 %copy-done.2 = f32[2,64,2048]{2,1,0:T(8,128)S(1)} copy-done((f32[2,64,2048]{2,1,0:T(8,128)S(1)}, f32[2,64,2048]{2,1,0:T(8,128)}, u32[]{:S(2)}) %copy-start.2) | copy-done | bytes 1048600
  1.2 0.0 copy-start.3
  1.2 1.2 %copy-done.3 = f32[512,512]{1,0:T(8,128)S(1)} copy-done((f32[512,512]{1,0:T(8,128)S(1)}, f32[512,512]{1,0:T(8,128)}, u32[]{:S(2)}) %copy-start.3) | copy-done | bytes 1048600
  2.5 0.0 copy-start.4
  2.5 0.7 copy-done.4
  3.1 0.0 copy-start.5
  3.1 0.7 copy-done.5
  3.8 6.7 %prepare.1 = (bf16[1024,512]{1,0:T(8,128)(2,1)S(1)}, bf16[32,512]{1,0:T(8,128)(2,1)S(1)}) custom-call(s32[2]{0:T(128)S(1)} %copy-done.4, f32[2,64,2048]{2,1,0:T(8,128)S(1)} %copy-done.2, s32[1,64]{1,0:T(1,128)S(1)} %bitcast.8, f32[512,512]{1,0:T(8,128)S(1)} %copy-done.3), custom_call_target="tpu_custom_call" | custom-call | tf_op jit(solution)/shard_map/prepare/pallas_call | solution.py:74
  10.5 58.9 %exchange.1 = (bf16[4,16,4,16,512]{4,3,2,1,0:T(8,128)(2,1)S(1)}, bf16[16,4,32,512]{3,2,1,0:T(8,128)(2,1)S(1)}) custom-call(bf16[16,4,16,512]{3,2,1,0:T(8,128)(2,1)S(1)} %bitcast.7, bf16[32,512]{1,0:T(8,128)(2,1)S(1)} %get-tuple-element.10.first), custom_call_target="tpu_custom_call" | custom-call | tf_op jit(solution)/shard_map/exchange/pallas_call | solution.py:309
  69.5 0.0 copy-start
  69.5 1.9 %copy-done = bf16[4,16,4,16,512]{4,3,2,1,0:T(8,128)(2,1)} copy-done((bf16[4,16,4,16,512]{4,3,2,1,0:T(8,128)(2,1)}, bf16[4,16,4,16,512]{4,3,2,1,0:T(8,128)(2,1)S(1)}, u32[]{:S(2)}) %copy-start) | copy-done | bytes 4194328
  71.4 0.0 copy-start.1
  71.4 1.3 %copy-done.1 = bf16[16,4,32,512]{3,2,1,0:T(8,128)(2,1)} copy-done((bf16[16,4,32,512]{3,2,1,0:T(8,128)(2,1)}, bf16[16,4,32,512]{3,2,1,0:T(8,128)(2,1)S(1)}, u32[]{:S(2)}) %copy-start.1) | copy-done | bytes 2097176
  72.7 30.6 %correlate.1 = bf16[64,128,512]{2,1,0:T(8,128)(2,1)} custom-call(bf16[4,64,16,512]{3,2,1,0:T(8,128)(2,1)} %bitcast.5, bf16[64,32,512]{2,1,0:T(8,128)(2,1)} %bitcast.6, bf16[512,512]{1,0:T(8,128)(2,1)} %constant.5.clone.inv), custom_call_target="tpu_custom_call" | custom-call | tf_op jit(solution)/shard_map/correlate/pallas_call | solution.py:386
Async XLA Ops:
  0.0 1.2 %copy-start.2 = (f32[2,64,2048]{2,1,0:T(8,128)S(1)}, f32[2,64,2048]{2,1,0:T(8,128)}, u32[]{:S(2)}) copy-start(f32[2,64,2048]{2,1,0:T(8,128)} %raw.1) | copy-start | bytes 3145732
  1.2 1.2 %copy-start.3 = (f32[512,512]{1,0:T(8,128)S(1)}, f32[512,512]{1,0:T(8,128)}, u32[]{:S(2)}) copy-start(f32[512,512]{1,0:T(8,128)} %constant.4.clone.table) | copy-start | bytes 3145732
  2.5 0.7 copy-start.4
  3.1 0.7 copy-start.5
  69.5 1.9 %copy-start = (bf16[4,16,4,16,512]{4,3,2,1,0:T(8,128)(2,1)}, bf16[4,16,4,16,512]{4,3,2,1,0:T(8,128)(2,1)S(1)}, u32[]{:S(2)}) copy-start(bf16[4,16,4,16,512]{4,3,2,1,0:T(8,128)(2,1)S(1)} %get-tuple-element.11) | copy-start | bytes 12582916
  71.4 1.3 %copy-start.1 = (bf16[16,4,32,512]{3,2,1,0:T(8,128)(2,1)}, bf16[16,4,32,512]{3,2,1,0:T(8,128)(2,1)S(1)}, u32[]{:S(2)}) copy-start(bf16[16,4,32,512]{3,2,1,0:T(8,128)(2,1)S(1)} %get-tuple-element.12) | copy-start | bytes 6291460

commit v2 on v1

--- a/solution.py
+++ b/solution.py
@@ -12,6 +12,10 @@
 WIN = 512
 NB = 128
 HALF = 256
+STEP = 72
+PITCH = 520
+NT = (((1,), (1,)), ((), ()))
+TN = (((0,), (0,)), ((), ()))
 
 
 def forward_table():
@@ -89,7 +93,7 @@
 ORDER = (2, 1, 3, 0)
 
 
-def exchange_kernel(slots, first, held, panels, staged, chunk, turn_send, turn_recv, xy_send, xy_recv, z_send, z_recv, pair_send, pair_recv,
+def exchange_kernel(slots, first, sources, receivers, held, panels, placed, turned, staged, chunk, turn_send, turn_recv, xy_send, xy_recv, z_send, z_recv, pair_send, pair_recv,
                     core_send, core_recv, pz_send, pz_recv, pxy_send, pxy_recv, local_sem):
     recv = lax.axis_index("recv")
     seg = lax.axis_index("seg")
@@ -157,6 +161,17 @@
             device_id_type=MESH,
         )
 
+    def core_arrival(turn, low):
+        place = held.at[low * 2 + 1 - core, :, (zh + 4 - turn) % 4]
+        return pltpu.make_async_remote_copy(
+            src_ref=place,
+            dst_ref=place,
+            send_sem=core_send.at[turn, low],
+            recv_sem=core_recv.at[turn, low],
+            device_id=(recv, seg),
+            device_id_type=MESH,
+        )
+
     def pz_copy(turn):
         return pltpu.make_async_remote_copy(
             src_ref=chunk,
@@ -186,6 +201,73 @@
             device_id=((seg * 4 + x) * 4 + zh, y),
             device_id_type=MESH,
         )
+
+    row = lax.broadcasted_iota(jnp.int32, (256, 256), 0)
+    column = lax.broadcasted_iota(jnp.int32, (256, 256), 1)
+
+    def zero_one(hits):
+        return hits.astype(jnp.float32).astype(jnp.bfloat16)
+
+    def place_block(window_group, block):
+        order = zero_one(row % 32 // 2 * 16 + row % 2 * 8 + row // 32 == column)
+        rows = jnp.dot(
+            order,
+            held[window_group, :, block].reshape(256, WIN),
+            preferred_element_type=jnp.float32,
+        ).astype(jnp.bfloat16)
+        for w in range(8):
+            start = (window_group * 8 + w) * 128 + block * 32
+            placed[pl.ds(pl.multiple_of(start, 32), 32), :] = rows[w * 32 : w * 32 + 32]
+
+    def turn_receivers():
+        channel = row % 128
+        order = zero_one(
+            (column // 128 == row // 128)
+            & (column % 128 == channel % 32 // 2 * 8 + channel // 32 * 2 + channel % 2)
+        )
+
+        @pl.loop(0, 16, unroll=2)
+        def _(n):
+            for c in range(2):
+                block = placed[pl.ds(pl.multiple_of(n * 256, 256), 256), c * HALF : c * HALF + HALF]
+                part = lax.dot_general(block, order, TN, preferred_element_type=jnp.float32)
+                for w in range(2):
+                    receivers[pl.ds(c * 32 + n * 2 + w, HALF, stride=STEP), :] = part[
+                        :, w * 128 : w * 128 + 128
+                    ]
+
+    def turn_sources(window_group):
+        order = zero_one(row % 16 // 2 * 32 + row % 32 // 16 * 16 + row % 2 * 8 + row // 32 == column)
+        same = zero_one(row == column)
+        low_lane = lax.broadcasted_iota(jnp.int32, (HALF, 128), 1) < 64
+        zero_row = lax.broadcasted_iota(jnp.int32, (HALF, 128), 0) == 0
+        for g in range(2):
+            block = panels[pl.ds(window_group * 4 + g * 2, 2)].reshape(256, WIN)
+            rows = jnp.dot(order, block, preferred_element_type=jnp.float32).astype(jnp.bfloat16)
+            for w in range(8):
+                for b in range(2):
+                    for copy in range(2):
+                        start = w * 128 + copy * 64 + b * 32 + g * 16
+                        turned[start : start + 16, :] = rows[w * 32 + b * 16 : w * 32 + b * 16 + 16]
+        for n in range(4):
+            real, imag = (
+                lax.dot_general(
+                    same,
+                    turned[n * 256 : n * 256 + 256, c * HALF : c * HALF + HALF],
+                    NT,
+                    preferred_element_type=jnp.float32,
+                )
+                for c in range(2)
+            )
+            for w in range(2):
+                re, im = real[:, w * 128 : w * 128 + 128], imag[:, w * 128 : w * 128 + 128]
+                window = window_group * 8 + n * 2 + w
+                sources[pl.ds(window, HALF, stride=STEP), :] = jnp.where(
+                    low_lane, re, jnp.where(zero_row, 0.0, -im)
+                )
+                sources[pl.ds(32 + window, HALF, stride=STEP), :] = jnp.where(
+                    low_lane, jnp.where(zero_row, 0.0, im), jnp.where(zero_row, im, re)
+                )
 
     barrier = pltpu.get_barrier_semaphore()
 
@@ -281,13 +363,32 @@
         core_copy(turn, low).start()
     z_arrival(0, 1 - zl).wait_recv()
     core_copy(0, 1 - zl).start()
-    for turn, low in ((2, zl), (far, 0), (far, 1)):
-        pair_copy(turn, low).wait_recv()
-        core_copy(turn, low).start()
 
     @pl.loop(1, 16)
     def _(step):
         pxy_copy(step).wait_recv()
+
+    @pl.loop(0, 4)
+    def _(window_group):
+        turn_sources(window_group)
+
+    early = ((0, zl), (2, 1 - zl), (direct, 0), (direct, 1), (0, 1 - zl))
+    late = ((2, zl), (far, 0), (far, 1))
+    for turn, low in early:
+        place_block(low * 2 + core, (zh + 4 - turn) % 4)
+    for turn, low in late:
+        pair_copy(turn, low).wait_recv()
+        core_copy(turn, low).start()
+    for turn, low in late:
+        place_block(low * 2 + core, (zh + 4 - turn) % 4)
+    for turn in range(4):
+        for low in (0, 1):
+            core_arrival(turn, low).wait_recv()
+            place_block(low * 2 + 1 - core, (zh + 4 - turn) % 4)
+    turn_receivers()
+
+    @pl.loop(1, 16)
+    def _(step):
         pxy_copy(step).wait_send()
         for turn in ORDER:
             xy_copy(turn, step).wait_send()
@@ -300,7 +401,7 @@
         pair_copy(turn, low).wait_send()
     for turn in range(4):
         for low in (0, 1):
-            core_copy(turn, low).wait()
+            core_copy(turn, low).wait_send()
 
 
 def exchange(slots, chunk):
@@ -309,12 +410,16 @@
     return pl.pallas_call(
         exchange_kernel,
         out_shape=(
-            jax.ShapeDtypeStruct((4, 16, 4, rows, width), jnp.bfloat16),
-            jax.ShapeDtypeStruct((16, 4) + chunk.shape, jnp.bfloat16),
+            jax.ShapeDtypeStruct((HALF * STEP, 128), jnp.float32),
+            jax.ShapeDtypeStruct((HALF * STEP, 128), jnp.float32),
         ),
         in_specs=[pl.BlockSpec(memory_space=pltpu.VMEM)] * 2,
         out_specs=(pl.BlockSpec(memory_space=pltpu.VMEM),) * 2,
         scratch_shapes=[
+            pltpu.VMEM((4, 16, 4, rows, width), jnp.bfloat16),
+            pltpu.VMEM((16, 4) + chunk.shape, jnp.bfloat16),
+            pltpu.VMEM((4096, width), jnp.bfloat16),
+            pltpu.VMEM((1024, width), jnp.bfloat16),
             pltpu.VMEM((4, 16, rows, width), jnp.bfloat16),
             pltpu.VMEM(chunk.shape, jnp.bfloat16),
             dma, dma, dma((4, 16)), dma((4, 16)), dma((4,)), dma((4, 2)), dma((4, 2)), dma((4, 2)),
@@ -322,83 +427,74 @@
             dma((4,)), dma((4,)), dma((16,)), dma((16,)), dma((7,)),
         ],
         compiler_params=pltpu.CompilerParams(
-            collective_id=0, has_side_effects=True, vmem_limit_bytes=32 * 1024 * 1024
+            collective_id=0, has_side_effects=True, vmem_limit_bytes=22 * 1024 * 1024
         ),
         name="exchange",
     )(slots, chunk)
 
 
-NT=(((1,),(1,)),((),())); TN=(((0,),(0,)),((),()))
-def body(held, panels, inv, out, x, rf, lt, ss, *, per):
-    f32=jnp.float32; bf=jnp.bfloat16
-    @pl.when(pl.program_id(0)==0)
-    def _():
-        row=lax.broadcasted_iota(jnp.int32,(256,256),0); col=lax.broadcasted_iota(jnp.int32,(256,256),1)
-        eye=(row==col).astype(f32).astype(bf)
-        def turned(n,c):
-            return lax.dot_general(eye, x[pl.ds(pl.multiple_of(n*256,256),256),c*256:(c+1)*256], NT, preferred_element_type=f32)
-        perm=((row%32)//2*16+row%2*8+row//32==col).astype(f32).astype(bf)
-        @pl.loop(0,16,unroll=2)
-        def _(n):
-            k=n//4; g=n%4
-            y=jnp.dot(perm, held[k,pl.ds(g*16,16)].reshape(256,512), preferred_element_type=f32).astype(bf)
-            for w in range(8):
-                x[pl.ds(pl.multiple_of((k*8+w)*128+g*32,32),32),:]=y[w*32:(w+1)*32]
-        @pl.loop(0,16,unroll=2)
-        def _(n):
-            for c in range(2):
-                v=turned(n,c)
-                for dw in range(2):
-                    rf[pl.ds(c*32+n*2+dw,256,stride=72),:]=v[:,dw*128:(dw+1)*128]
-        perm2=((row%16)//2*32+(row%32)//16*16+row%2*8+row//32==col).astype(f32).astype(bf)
-        @pl.loop(0,8,unroll=2)
-        def _(n):
-            k=n//2; g=n%2
-            y=jnp.dot(perm2, panels[pl.ds(n*8,8)].reshape(256,512), preferred_element_type=f32).astype(bf)
-            for w in range(8):
-                for b in range(2):
-                    for h in range(2):
-                        x[pl.ds(pl.multiple_of((k*8+w)*128+h*64+b*32+g*16,16),16),:]=y[w*32+b*16:w*32+b*16+16]
-        lane=lax.broadcasted_iota(jnp.int32,(256,128),1)<64
-        first=lax.broadcasted_iota(jnp.int32,(256,128),0)==0
-        @pl.loop(0,16,unroll=2)
-        def _(n):
-            real, imag = turned(n,0), turned(n,1)
-            for dw in range(2):
-                re=real[:,dw*128:(dw+1)*128]; im=imag[:,dw*128:(dw+1)*128]
-                lt[pl.ds(n*2+dw,256,stride=72),:]=jnp.where(lane,re,jnp.where(first,0.0,-im))
-                lt[pl.ds(32+n*2+dw,256,stride=72),:]=jnp.where(lane,jnp.where(first,0.0,im),jnp.where(first,im,re))
-        @pl.loop(0,256,unroll=8)
-        def _(j):
-            at=pl.ds(pl.multiple_of(j*72,8),64)
-            s=lax.dot_general(lt[at,:].astype(bf), rf[at,:].astype(bf), TN, preferred_element_type=f32)
-            ss[pl.ds(j,64,stride=520),:]=s[:64]
-            ss[pl.ds(256+j,64,stride=520),:]=s[64:]
-    base=pl.program_id(0)*per
-    @pl.loop(0,per,unroll=4)
-    def _(i):
-        v=ss[pl.ds(pl.multiple_of((base+i)*520,8),512),:].astype(bf)
-        out[i]=lax.dot_general(v, inv[...], TN, preferred_element_type=f32).astype(bf)
-
-def compute(held, panels, inv, per=8):
-    one=pl.Buffered(1)
-    def whole(a): return pl.BlockSpec(a.shape, lambda i: (0,)*a.ndim, pipeline_mode=one)
-    return pl.pallas_call(functools.partial(body,per=per), grid=(64//per,),
-        out_shape=jax.ShapeDtypeStruct((64,128,512),jnp.bfloat16),
-        in_specs=[whole(held),whole(panels),whole(inv)],
-        out_specs=pl.BlockSpec((per,128,512),lambda i:(i,0,0)),
-        scratch_shapes=[pltpu.VMEM((4096,512),jnp.bfloat16),pltpu.VMEM((256*72,128),jnp.float32),
-            pltpu.VMEM((256*72,128),jnp.float32),pltpu.VMEM((64*520,128),jnp.float32)],
-        compiler_params=pltpu.CompilerParams(vmem_limit_bytes=56*1024*1024), name="correlate")(held,panels,inv)
+def correlate_kernel(sources, receivers, inverse, out, stack, lagged, sent):
+    @pl.loop(0, HALF, unroll=8)
+    def _(j):
+        at = pl.ds(pl.multiple_of(j * STEP, 8), 64)
+        terms = lax.dot_general(
+            sources[at, :].astype(jnp.bfloat16),
+            receivers[at, :].astype(jnp.bfloat16),
+            TN,
+            preferred_element_type=jnp.float32,
+        )
+        stack[pl.ds(j, 64, stride=PITCH), :] = terms[:64]
+        stack[pl.ds(HALF + j, 64, stride=PITCH), :] = terms[64:]
+
+    def out_copy(group, slot):
+        return pltpu.make_async_copy(lagged.at[slot], out.at[pl.ds(group * 8, 8)], sent.at[slot])
+
+    @pl.loop(0, 4)
+    def _(pair):
+        for slot in range(2):
+            group = pair * 2 + slot
+
+            @pl.when(pair > 0)
+            def _():
+                out_copy(group - 2, slot).wait()
+
+            @pl.loop(0, 8, unroll=4)
+            def _(i):
+                start = (group * 8 + i) * PITCH
+                lagged[slot, i] = lax.dot_general(
+                    stack[pl.ds(pl.multiple_of(start, 8), WIN), :].astype(jnp.bfloat16),
+                    inverse[...],
+                    TN,
+                    preferred_element_type=jnp.float32,
+                ).astype(jnp.bfloat16)
+
+            out_copy(group, slot).start()
+
+    for slot in range(2):
+        out_copy(6 + slot, slot).wait()
+
+
+def correlate(sources, receivers, inverse):
+    return pl.pallas_call(
+        correlate_kernel,
+        out_shape=jax.ShapeDtypeStruct((64, 128, WIN), jnp.bfloat16),
+        in_specs=[pl.BlockSpec(memory_space=pltpu.VMEM)] * 3,
+        out_specs=pl.BlockSpec(memory_space=pl.ANY),
+        scratch_shapes=[
+            pltpu.VMEM((64 * PITCH, 128), jnp.float32),
+            pltpu.VMEM((2, 8, 128, WIN), jnp.bfloat16),
+            pltpu.SemaphoreType.DMA((2,)),
+        ],
+        compiler_params=pltpu.CompilerParams(vmem_limit_bytes=24 * 1024 * 1024),
+        name="correlate",
+    )(sources, receivers, inverse)
 
 
 def local(raw_data, row_owner, source_blocks):
     slots, chunk = prepare(raw_data, row_owner, source_blocks)
-    held, panels = exchange(slots.reshape(16, 4, 16, WIN), chunk)
+    sources, receivers = exchange(slots.reshape(16, 4, 16, WIN), chunk)
     inverse = jnp.asarray(inverse_table(32), jnp.bfloat16)
-    lagged = compute(
-        held.reshape(4, 64, 16, WIN), panels.reshape(64, 32, WIN), inverse
-    )
+    lagged = correlate(sources, receivers, inverse)
     return lagged.reshape(2, 32, 128, WIN)
 
 

time: 103 us -> 96.7 us (0.939)
  the two profiles are of different devices: /device:TPU:1 before, /device:TPU:33 now
where the time goes in v2:
time: 96.7 us; the launch traced here: 96.4 us
  Pallas kernels  91.6 us (95%)
  local copies, waits for them, and re-layouts  4.8 us (5%)
    pallas_call x1, Pallas kernels, exchange(): pl.pallas_call(exchange_kernel, out_shape=(jax.ShapeDtypeStruct((HALF * S...  67.6 us
    pallas_call x1, Pallas kernels, correlate(): pl.pallas_call(correlate_kernel, out_shape=jax.ShapeDtypeStruct((64, 128,...  17.3 us
    pallas_call x1, Pallas kernels, prepare(): pl.pallas_call(prepare_kernel, out_shape=(jax.ShapeDtypeStruct((1024, WIN...  6.74 us
    unnamed x10, local copies, waits for them, and re-layouts  4.8 us

profile of v2, /device:TPU:33, one launch (start us, length us, event | category | flops | bytes accessed | tf_op | source)
XLA Modules:
  0.0 96.4 jit_solution(7995279261303127067)
XLA Ops:
  0.0 0.0 copy-start
  0.0 1.2 %copy-done = f32[2,64,2048]{2,1,0:T(8,128)S(1)} copy-done((f32[2,64,2048]{2,1,0:T(8,128)S(1)}, f32[2,64,2048]{2,1,0:T(8,128)}, u32[]{:S(2)}) %copy-start) | copy-done | bytes 1048600
  1.2 0.0 copy-start.1
  1.2 1.2 %copy-done.1 = f32[512,512]{1,0:T(8,128)S(1)} copy-done((f32[512,512]{1,0:T(8,128)S(1)}, f32[512,512]{1,0:T(8,128)}, u32[]{:S(2)}) %copy-start.1) | copy-done | bytes 1048600
  2.5 0.0 copy-start.3
  2.5 0.7 copy-done.3
  3.1 0.0 copy-start.4
  3.1 0.7 copy-done.4
  3.8 6.7 %prepare.1 = (bf16[1024,512]{1,0:T(8,128)(2,1)S(1)}, bf16[32,512]{1,0:T(8,128)(2,1)S(1)}) custom-call(s32[2]{0:T(128)S(1)} %copy-done.3, f32[2,64,2048]{2,1,0:T(8,128)S(1)} %copy-done, s32[1,64]{1,0:T(1,128)S(1)} %bitcast.4, f32[512,512]{1,0:T(8,128)S(1)} %copy-done.1), custom_call_target="tpu_custom_call" | custom-call | tf_op jit(solution)/shard_map/prepare/pallas_call | solution.py:78
  10.5 67.6 %exchange.1 = (f32[18432,128]{1,0:T(8,128)S(1)}, f32[18432,128]{1,0:T(8,128)S(1)}) custom-call(bf16[16,4,16,512]{3,2,1,0:T(8,128)(2,1)S(1)} %bitcast.3, bf16[32,512]{1,0:T(8,128)(2,1)S(1)} %get-tuple-element.10.first), custom_call_target="tpu_custom_call" | custom-call | tf_op jit(solution)/shard_map/exchange/pallas_call | solution.py:410
  78.1 0.0 copy-start.2
  78.1 1.0 %copy-done.2 = bf16[512,512]{1,0:T(8,128)(2,1)S(1)} copy-done((bf16[512,512]{1,0:T(8,128)(2,1)S(1)}, bf16[512,512]{1,0:T(8,128)(2,1)}, u32[]{:S(2)}) %copy-start.2) | copy-done | bytes 524312
  79.2 17.3 %correlate.1 = bf16[64,128,512]{2,1,0:T(8,128)(2,1)} custom-call(f32[18432,128]{1,0:T(8,128)S(1)} %get-tuple-element.11.sources, f32[18432,128]{1,0:T(8,128)S(1)} %get-tuple-element.12.receivers, bf16[512,512]{1,0:T(8,128)(2,1)S(1)} %copy-done.2), custom_call_target="tpu_custom_call" | custom-call | tf_op jit(solution)/shard_map/correlate/pallas_call | solution.py:478
Async XLA Ops:
  0.0 1.2 %copy-start = (f32[2,64,2048]{2,1,0:T(8,128)S(1)}, f32[2,64,2048]{2,1,0:T(8,128)}, u32[]{:S(2)}) copy-start(f32[2,64,2048]{2,1,0:T(8,128)} %raw.1) | copy-start | bytes 3145732
  1.2 1.2 %copy-start.1 = (f32[512,512]{1,0:T(8,128)S(1)}, f32[512,512]{1,0:T(8,128)}, u32[]{:S(2)}) copy-start(f32[512,512]{1,0:T(8,128)} %constant.4.clone.table) | copy-start | bytes 3145732
  2.5 0.7 copy-start.3
  3.1 0.7 copy-start.4
  78.1 1.0 %copy-start.2 = (bf16[512,512]{1,0:T(8,128)(2,1)S(1)}, bf16[512,512]{1,0:T(8,128)(2,1)}, u32[]{:S(2)}) copy-start(bf16[512,512]{1,0:T(8,128)(2,1)} %constant.5.clone.inverse) | copy-start | bytes 1572868

commit v3 on v2

--- a/solution.py
+++ b/solution.py
@@ -3,6 +3,7 @@
 
 import jax
 import jax.numpy as jnp
+import ml_dtypes
 import numpy as np
 from jax import lax
 from jax.experimental import pallas as pl
@@ -37,15 +38,62 @@
     return np.concatenate([cosine_rows, sine_rows], axis=0)
 
 
-def prepare_kernel(blocks, raw, owner, table, slots, chunk, spectra):
+def forward_halves():
+    table = forward_table().astype(np.float32)
+    high = table.astype(ml_dtypes.bfloat16)
+    low = (table - high.astype(np.float32)).astype(ml_dtypes.bfloat16)
+    return jnp.asarray(np.stack([high, low]))
+
+
+ORDER = (2, 1, 3, 0)
+GROUPS = ((0, 1), (1, 1), (2, 2))
+
+
+def split(values):
+    high = values.astype(jnp.bfloat16)
+    return high, (values - high.astype(jnp.float32)).astype(jnp.bfloat16)
+
+
+def product(left, right):
+    return jnp.dot(left, right, preferred_element_type=jnp.float32)
+
+
+def place_of(turn):
+    place = 0
+    for number, listed in enumerate(ORDER):
+        place = place + number * (turn == listed).astype(jnp.int32)
+    return place
+
+
+def prepare_kernel(blocks_hbm, raw_hbm, owner_hbm, table_hbm, slots, chunk, blocks, raw, owner, table, spectra, sems):
+    copies = [
+        pltpu.make_async_copy(owner_hbm, owner, sems.at[0]),
+        pltpu.make_async_copy(blocks_hbm, blocks, sems.at[1]),
+        pltpu.make_async_copy(table_hbm.at[0], table.at[0], sems.at[2]),
+        pltpu.make_async_copy(table_hbm.at[1], table.at[1], sems.at[3]),
+    ]
+    for piece in range(4):
+        rows = pl.ds(piece % 2 * 32, 32)
+        copies.append(
+            pltpu.make_async_copy(
+                raw_hbm.at[piece // 2, rows], raw.at[piece // 2, rows], sems.at[4 + piece]
+            )
+        )
+    for copy in copies:
+        copy.start()
+    zh = lax.axis_index("recv") % 4
     row = lax.broadcasted_iota(jnp.int32, (64, 512), 0)
     lane = lax.broadcasted_iota(jnp.int32, (64, 512), 1)
     diagonal = row[:, :64] == lane[:, :64]
+    copies[0].wait()
     owner_column = jnp.sum(jnp.where(diagonal, owner[...], 0), axis=1, keepdims=True)
     owner_row = jnp.sum(jnp.where(row == lane % 64, owner_column, 0), axis=0, keepdims=True)
     same = (owner_column == owner_row) & (row < lane % 64)
     rank = jnp.sum(same.astype(jnp.int32), axis=0, keepdims=True)
-    target = (owner_row * 2 + rank) * 8 + lax.broadcasted_iota(jnp.int32, (1, 512), 1) // 64
+    place = owner_row // 4 * 4 + place_of((owner_row % 4 + 4 - zh) % 4)
+    target = (place * 2 + rank) * 8 + lax.broadcasted_iota(jnp.int32, (1, 512), 1) // 64
+    for copy in copies[1:]:
+        copy.wait()
     for window in range(8):
         parts = []
         for run in range(4):
@@ -53,27 +101,26 @@
             values = raw[window // 4, :, start : start + NB]
             amplitude = jnp.mean(jnp.abs(values), axis=-1, keepdims=True) + 1e-06
             parts.append(values / amplitude)
-        spectra[window * 64 : window * 64 + 64, :] = jnp.dot(
-            jnp.concatenate(parts, axis=1),
-            table[...],
-            precision=lax.Precision.HIGHEST,
-            preferred_element_type=jnp.float32,
+        high, low = split(jnp.concatenate(parts, axis=1))
+        spectra[window * 64 : window * 64 + 64, :] = (
+            product(high, table[0]) + (product(low, table[0]) + product(high, table[1]))
         ).astype(jnp.bfloat16)
 
-    @pl.loop(0, 4)
+    @pl.loop(0, 4, unroll=2)
     def _(part):
         placed = lax.broadcasted_iota(jnp.int32, (256, 512), 0) + part * 256 == target
-        slots[pl.ds(pl.multiple_of(part * 256, 256), 256), :] = jnp.dot(
-            placed.astype(jnp.float32).astype(jnp.bfloat16),
-            spectra[...],
-            preferred_element_type=jnp.float32,
+        slots[pl.ds(pl.multiple_of(part * 256, 256), 256), :] = product(
+            placed.astype(jnp.float32).astype(jnp.bfloat16), spectra[...]
         ).astype(jnp.bfloat16)
 
     for b in range(2):
-        chunk[b * 16 : b * 16 + 16, :] = slots[pl.ds(pl.multiple_of(blocks[b] * 16, 16), 16), :]
+        block = blocks[b]
+        start = (block // 4 * 4 + place_of((block % 4 + 4 - zh) % 4)) * 16
+        chunk[b * 16 : b * 16 + 16, :] = slots[pl.ds(pl.multiple_of(start, 16), 16), :]
 
 
 def prepare(raw_data, row_owner, source_blocks):
+    hbm = pl.BlockSpec(memory_space=pltpu.HBM)
     vmem = pl.BlockSpec(memory_space=pltpu.VMEM)
     return pl.pallas_call(
         prepare_kernel,
@@ -81,16 +128,22 @@
             jax.ShapeDtypeStruct((1024, WIN), jnp.bfloat16),
             jax.ShapeDtypeStruct((32, WIN), jnp.bfloat16),
         ),
-        in_specs=[pl.BlockSpec(memory_space=pltpu.SMEM), vmem, vmem, vmem],
+        in_specs=[hbm] * 4,
         out_specs=(vmem, vmem),
-        scratch_shapes=[pltpu.VMEM((512, WIN), jnp.bfloat16)],
-        compiler_params=pltpu.CompilerParams(vmem_limit_bytes=24 * 1024 * 1024),
+        scratch_shapes=[
+            pltpu.SMEM((2,), jnp.int32),
+            pltpu.VMEM(raw_data.shape, jnp.float32),
+            pltpu.VMEM((1, 64), jnp.int32),
+            pltpu.VMEM((2, WIN, WIN), jnp.bfloat16),
+            pltpu.VMEM((512, WIN), jnp.bfloat16),
+            pltpu.SemaphoreType.DMA((8,)),
+        ],
+        compiler_params=pltpu.CompilerParams(vmem_limit_bytes=60 * 1024 * 1024),
         name="prepare",
-    )(source_blocks, raw_data, row_owner.reshape(1, 64), jnp.asarray(forward_table(), jnp.float32))
+    )(source_blocks, raw_data, row_owner.reshape(1, 64), forward_halves())
 
 
 MESH = pl.DeviceIdType.MESH
-ORDER = (2, 1, 3, 0)
 
 
 def exchange_kernel(slots, first, sources, receivers, held, panels, placed, turned, staged, chunk, turn_send, turn_recv, xy_send, xy_recv, z_send, z_recv, pair_send, pair_recv,
@@ -104,70 +157,76 @@
     def plane_peer(step):
         return ((y + step // 4) % 4) * 4 + (x + step % 4) % 4
 
-    def xy_copy(turn, step):
+    def xy_copy(group, step):
         target = plane_peer(step)
-        block = (zh + turn) % 4
-        return pltpu.make_async_remote_copy(
-            src_ref=slots.at[target, block],
-            dst_ref=staged.at[block, plane],
-            send_sem=xy_send.at[turn, step],
-            recv_sem=xy_recv.at[turn, step],
+        start, count = GROUPS[group]
+        places = pl.ds(start, count)
+        return pltpu.make_async_remote_copy(
+            src_ref=slots.at[target, places],
+            dst_ref=staged.at[places, plane],
+            send_sem=xy_send.at[group, step],
+            recv_sem=xy_recv.at[group, step],
             device_id=(target * 4 + zh, seg),
             device_id_type=MESH,
         )
 
     near = (None, 0, 1 - zl, 1)
 
-    def z_copy(turn, low):
-        block = (zh + turn) % 4
-        return pltpu.make_async_remote_copy(
-            src_ref=staged.at[block],
-            dst_ref=held.at[seg, :, zh],
-            send_sem=z_send.at[turn],
-            recv_sem=z_recv.at[turn, zl],
-            device_id=(plane * 4 + block, low * 2 + core),
-            device_id_type=MESH,
-        )
-
-    def z_arrival(turn, low):
-        return pltpu.make_async_remote_copy(
-            src_ref=staged.at[0],
-            dst_ref=held.at[low * 2 + core, :, (zh + 4 - turn) % 4],
-            send_sem=z_send.at[turn],
-            recv_sem=z_recv.at[turn, low],
+    def half_of(half):
+        return pl.ds(half * 8, 8)
+
+    def held_from(turn, low, owner_core, half):
+        return held.at[low * 2 + owner_core, half_of(half), (zh + 4 - turn) % 4]
+
+    def z_copy(turn, low, half):
+        return pltpu.make_async_remote_copy(
+            src_ref=staged.at[ORDER.index(turn), half_of(half)],
+            dst_ref=held.at[seg, half_of(half), zh],
+            send_sem=z_send.at[turn, half],
+            recv_sem=z_recv.at[turn, zl, half],
+            device_id=(plane * 4 + (zh + turn) % 4, low * 2 + core),
+            device_id_type=MESH,
+        )
+
+    def z_arrival(turn, low, half):
+        return pltpu.make_async_remote_copy(
+            src_ref=staged.at[0, half_of(half)],
+            dst_ref=held_from(turn, low, core, half),
+            send_sem=z_send.at[turn, half],
+            recv_sem=z_recv.at[turn, low, half],
             device_id=(recv, seg),
             device_id_type=MESH,
         )
 
-    def pair_copy(turn, low):
-        place = held.at[low * 2 + core, :, (zh + 4 - turn) % 4]
+    def pair_copy(turn, low, half):
+        place = held_from(turn, low, core, half)
         return pltpu.make_async_remote_copy(
             src_ref=place,
             dst_ref=place,
-            send_sem=pair_send.at[turn, low],
-            recv_sem=pair_recv.at[turn, low],
+            send_sem=pair_send.at[turn, low, half],
+            recv_sem=pair_recv.at[turn, low, half],
             device_id=(recv, (1 - zl) * 2 + core),
             device_id_type=MESH,
         )
 
-    def core_copy(turn, low):
-        place = (zh + 4 - turn) % 4
-        return pltpu.make_async_remote_copy(
-            src_ref=held.at[low * 2 + core, :, place],
-            dst_ref=held.at[low * 2 + core, :, place],
-            send_sem=core_send.at[turn, low],
-            recv_sem=core_recv.at[turn, low],
-            device_id=(recv, zl * 2 + 1 - core),
-            device_id_type=MESH,
-        )
-
-    def core_arrival(turn, low):
-        place = held.at[low * 2 + 1 - core, :, (zh + 4 - turn) % 4]
+    def core_copy(turn, low, half):
+        place = held_from(turn, low, core, half)
         return pltpu.make_async_remote_copy(
             src_ref=place,
             dst_ref=place,
-            send_sem=core_send.at[turn, low],
-            recv_sem=core_recv.at[turn, low],
+            send_sem=core_send.at[turn, low, half],
+            recv_sem=core_recv.at[turn, low, half],
+            device_id=(recv, zl * 2 + 1 - core),
+            device_id_type=MESH,
+        )
+
+    def core_arrival(turn, low, half):
+        place = held_from(turn, low, 1 - core, half)
+        return pltpu.make_async_remote_copy(
+            src_ref=place,
+            dst_ref=place,
+            send_sem=core_send.at[turn, low, half],
+            recv_sem=core_recv.at[turn, low, half],
             device_id=(recv, seg),
             device_id_type=MESH,
         )
@@ -294,11 +353,9 @@
     def _():
         kept_chunk.start()
 
-    own = []
-    for turn in ORDER:
-        block = (zh + turn) % 4
-        own.append(pltpu.make_async_copy(slots.at[plane, block], staged.at[block, plane], local_sem.at[turn]))
-        own[-1].start()
+    own = pltpu.make_async_copy(slots.at[plane], staged.at[:, plane], local_sem.at[0])
+    own.start()
+
     @pl.when(y == seg)
     def _():
         pl.semaphore_wait(barrier, 23)
@@ -308,14 +365,11 @@
         pl.semaphore_wait(barrier, 24)
         turn_copy().start()
 
-    for turn in ORDER[:1]:
+    for group in range(len(GROUPS)):
+
         @pl.loop(1, 16)
         def _(step):
-            xy_copy(turn, step).start()
-    for turn in ORDER[1:]:
-        @pl.loop(1, 16)
-        def _(step):
-            xy_copy(turn, step).start()
+            xy_copy(group, step).start()
 
     @pl.when(y != seg)
     def _():
@@ -329,23 +383,20 @@
     for turn in (1, 2, 3):
         pz_copy(turn).start()
 
-    kept = None
-    for number, turn in enumerate(ORDER):
-        own[number].wait()
+    kept = pltpu.make_async_copy(staged.at[ORDER.index(0)], held.at[seg, :, zh], local_sem.at[5])
+    own.wait()
+    for group, (start, count) in enumerate(GROUPS):
 
         @pl.loop(1, 16)
         def _(step):
-            xy_copy(turn, step).wait_recv()
-
-        if turn:
-            z_copy(turn, near[turn]).start()
-        else:
-            z_copy(0, 1 - zl).start()
-            kept = pltpu.make_async_copy(
-                staged.at[zh], held.at[seg, :, zh], local_sem.at[5]
-            )
-            kept.start()
-        if number == 0:
+            xy_copy(group, step).wait_recv()
+
+        for turn in ORDER[start : start + count]:
+            for half in range(2):
+                z_copy(turn, near[turn] if turn else 1 - zl, half).start()
+            if not turn:
+                kept.start()
+        if group == 0:
             own_chunk.wait()
             for other in (1, 2, 3):
                 pz_copy(other).wait_recv()
@@ -355,53 +406,61 @@
                 pxy_copy(step).start()
 
     kept.wait()
-    core_copy(0, zl).start()
+    for half in range(2):
+        core_copy(0, zl, half).start()
     direct, far = 1 + 2 * zl, 3 - 2 * zl
     for turn, low in ((2, 1 - zl), (direct, 0), (direct, 1)):
-        z_arrival(turn, low).wait_recv()
-        pair_copy(turn, low).start()
-        core_copy(turn, low).start()
-    z_arrival(0, 1 - zl).wait_recv()
-    core_copy(0, 1 - zl).start()
-
-    @pl.loop(1, 16)
-    def _(step):
-        pxy_copy(step).wait_recv()
-
-    @pl.loop(0, 4)
-    def _(window_group):
-        turn_sources(window_group)
+        for half in range(2):
+            z_arrival(turn, low, half).wait_recv()
+            pair_copy(turn, low, half).start()
+            core_copy(turn, low, half).start()
+    for half in range(2):
+        z_arrival(0, 1 - zl, half).wait_recv()
+        core_copy(0, 1 - zl, half).start()
 
     early = ((0, zl), (2, 1 - zl), (direct, 0), (direct, 1), (0, 1 - zl))
     late = ((2, zl), (far, 0), (far, 1))
     for turn, low in early:
         place_block(low * 2 + core, (zh + 4 - turn) % 4)
+    for turn, low in early:
+        for half in range(2):
+            core_arrival(turn, low, half).wait_recv()
+        place_block(low * 2 + 1 - core, (zh + 4 - turn) % 4)
+
+    @pl.loop(1, 16)
+    def _(step):
+        pxy_copy(step).wait_recv()
+
+    @pl.loop(0, 4)
+    def _(window_group):
+        turn_sources(window_group)
+
     for turn, low in late:
-        pair_copy(turn, low).wait_recv()
-        core_copy(turn, low).start()
+        for half in range(2):
+            pair_copy(turn, low, half).wait_recv()
+            core_copy(turn, low, half).start()
+        place_block(low * 2 + core, (zh + 4 - turn) % 4)
     for turn, low in late:
-        place_block(low * 2 + core, (zh + 4 - turn) % 4)
-    for turn in range(4):
-        for low in (0, 1):
-            core_arrival(turn, low).wait_recv()
-            place_block(low * 2 + 1 - core, (zh + 4 - turn) % 4)
+        for half in range(2):
+            core_arrival(turn, low, half).wait_recv()
+        place_block(low * 2 + 1 - core, (zh + 4 - turn) % 4)
     turn_receivers()
 
     @pl.loop(1, 16)
     def _(step):
         pxy_copy(step).wait_send()
-        for turn in ORDER:
-            xy_copy(turn, step).wait_send()
+        for group in range(len(GROUPS)):
+            xy_copy(group, step).wait_send()
 
     for turn in (1, 2, 3):
         pz_copy(turn).wait_send()
-        z_copy(turn, near[turn]).wait_send()
-    z_copy(0, 1 - zl).wait_send()
-    for turn, low in ((2, 1 - zl), (direct, 0), (direct, 1)):
-        pair_copy(turn, low).wait_send()
-    for turn in range(4):
-        for low in (0, 1):
-            core_copy(turn, low).wait_send()
+    for half in range(2):
+        for turn in range(4):
+            z_copy(turn, near[turn] if turn else 1 - zl, half).wait_send()
+            for low in (0, 1):
+                core_copy(turn, low, half).wait_send()
+        for turn, low in ((2, 1 - zl), (direct, 0), (direct, 1)):
+            pair_copy(turn, low, half).wait_send()
 
 
 def exchange(slots, chunk):
@@ -422,8 +481,8 @@
             pltpu.VMEM((1024, width), jnp.bfloat16),
             pltpu.VMEM((4, 16, rows, width), jnp.bfloat16),
             pltpu.VMEM(chunk.shape, jnp.bfloat16),
-            dma, dma, dma((4, 16)), dma((4, 16)), dma((4,)), dma((4, 2)), dma((4, 2)), dma((4, 2)),
-            dma((4, 2)), dma((4, 2)),
+            dma, dma, dma((4, 16)), dma((4, 16)), dma((4, 2)), dma((4, 2, 2)),
+            dma((4, 2, 2)), dma((4, 2, 2)), dma((4, 2, 2)), dma((4, 2, 2)),
             dma((4,)), dma((4,)), dma((16,)), dma((16,)), dma((7,)),
         ],
         compiler_params=pltpu.CompilerParams(
@@ -433,7 +492,10 @@
     )(slots, chunk)
 
 
-def correlate_kernel(sources, receivers, inverse, out, stack, lagged, sent):
+def correlate_kernel(sources, receivers, inverse_hbm, out, stack, lagged, inverse, sent):
+    table_copy = pltpu.make_async_copy(inverse_hbm, inverse, sent.at[2])
+    table_copy.start()
+
     @pl.loop(0, HALF, unroll=8)
     def _(j):
         at = pl.ds(pl.multiple_of(j * STEP, 8), 64)
@@ -448,6 +510,8 @@
 
     def out_copy(group, slot):
         return pltpu.make_async_copy(lagged.at[slot], out.at[pl.ds(group * 8, 8)], sent.at[slot])
+
+    table_copy.wait()
 
     @pl.loop(0, 4)
     def _(pair):
@@ -478,12 +542,13 @@
     return pl.pallas_call(
         correlate_kernel,
         out_shape=jax.ShapeDtypeStruct((64, 128, WIN), jnp.bfloat16),
-        in_specs=[pl.BlockSpec(memory_space=pltpu.VMEM)] * 3,
+        in_specs=[pl.BlockSpec(memory_space=pltpu.VMEM)] * 2 + [pl.BlockSpec(memory_space=pltpu.HBM)],
         out_specs=pl.BlockSpec(memory_space=pl.ANY),
         scratch_shapes=[
             pltpu.VMEM((64 * PITCH, 128), jnp.float32),
             pltpu.VMEM((2, 8, 128, WIN), jnp.bfloat16),
-            pltpu.SemaphoreType.DMA((2,)),
+            pltpu.VMEM((WIN, WIN), jnp.bfloat16),
+            pltpu.SemaphoreType.DMA((3,)),
         ],
         compiler_params=pltpu.CompilerParams(vmem_limit_bytes=24 * 1024 * 1024),
         name="correlate",

time: 96.7 us -> 90.1 us (0.932)
  the two profiles are of different devices: /device:TPU:33 before, /device:TPU:1 now
where the time goes in v3:
time: 90.1 us; the launch traced here: 89.3 us
  Pallas kernels  86.2 us (96%)
  local copies, waits for them, and re-layouts  3.01 us (3%)
    pallas_call x1, Pallas kernels, exchange(): pl.pallas_call(exchange_kernel, out_shape=(jax.ShapeDtypeStruct((HALF * S...  63.1 us
    pallas_call x1, Pallas kernels, correlate(): pl.pallas_call(correlate_kernel, out_shape=jax.ShapeDtypeStruct((64, 128,...  17.3 us
    pallas_call x1, Pallas kernels, prepare(): pl.pallas_call(prepare_kernel, out_shape=(jax.ShapeDtypeStruct((1024, WIN...  5.8 us
    unnamed x6, local copies, waits for them, and re-layouts  3.01 us

profile of v3, /device:TPU:1, one launch (start us, length us, event | category | flops | bytes accessed | tf_op | source)
XLA Modules:
  0.0 89.3 jit_solution(3484233473454908193)
XLA Ops:
  0.0 5.8 %prepare.1 = (bf16[1024,512]{1,0:T(8,128)(2,1)}, bf16[32,512]{1,0:T(8,128)(2,1)}) custom-call(s32[2]{0:T(128)} %blocks_hbm.1, f32[2,64,2048]{2,1,0:T(8,128)} %raw_hbm.1, s32[1,64]{1,0:T(1,128)} %bitcast.4, bf16[2,512,512]{2,1,0:T(8,128)(2,1)} %constant.4.clone.table_hbm), custom_call_target="tpu_custom_call" | custom-call | tf_op jit(solution)/shard_map/prepare/pallas_call | solution.py:125
  5.8 0.0 copy-start
  5.8 1.2 %copy-done = bf16[1024,512]{1,0:T(8,128)(2,1)S(1)} copy-done((bf16[1024,512]{1,0:T(8,128)(2,1)S(1)}, bf16[1024,512]{1,0:T(8,128)(2,1)}, u32[]{:S(2)}) %copy-start) | copy-done | bytes 1048600
  7.0 0.0 copy-start.2
  7.0 0.8 copy-done.2
  7.8 63.1 %exchange.1 = (f32[18432,128]{1,0:T(8,128)S(1)}, f32[18432,128]{1,0:T(8,128)S(1)}) custom-call(bf16[16,4,16,512]{3,2,1,0:T(8,128)(2,1)S(1)} %bitcast.3, bf16[32,512]{1,0:T(8,128)(2,1)S(1)} %copy-done.2), custom_call_target="tpu_custom_call" | custom-call | tf_op jit(solution)/shard_map/exchange/pallas_call | solution.py:469
  70.9 0.0 copy-start.1
  70.9 1.0 %copy-done.1 = bf16[512,512]{1,0:T(8,128)(2,1)S(1)} copy-done((bf16[512,512]{1,0:T(8,128)(2,1)S(1)}, bf16[512,512]{1,0:T(8,128)(2,1)}, u32[]{:S(2)}) %copy-start.1) | copy-done | bytes 524312
  71.9 17.3 %correlate.1 = bf16[64,128,512]{2,1,0:T(8,128)(2,1)} custom-call(f32[18432,128]{1,0:T(8,128)S(1)} %get-tuple-element.11.sources, f32[18432,128]{1,0:T(8,128)S(1)} %get-tuple-element.12.receivers, bf16[512,512]{1,0:T(8,128)(2,1)S(1)} %copy-done.1), custom_call_target="tpu_custom_call" | custom-call | tf_op jit(solution)/shard_map/correlate/pallas_call | solution.py:542
Async XLA Ops:
  5.8 1.2 %copy-start = (bf16[1024,512]{1,0:T(8,128)(2,1)S(1)}, bf16[1024,512]{1,0:T(8,128)(2,1)}, u32[]{:S(2)}) copy-start(bf16[1024,512]{1,0:T(8,128)(2,1)} %get-tuple-element.9) | copy-start | bytes 3145732
  7.0 0.8 copy-start.2
  70.9 1.0 %copy-start.1 = (bf16[512,512]{1,0:T(8,128)(2,1)S(1)}, bf16[512,512]{1,0:T(8,128)(2,1)}, u32[]{:S(2)}) copy-start(bf16[512,512]{1,0:T(8,128)(2,1)} %constant.5.clone.inverse_hbm) | copy-start | bytes 1572868

commit v4 on v3

--- a/solution.py
+++ b/solution.py
@@ -65,7 +65,7 @@
     return place
 
 
-def prepare_kernel(blocks_hbm, raw_hbm, owner_hbm, table_hbm, slots, chunk, blocks, raw, owner, table, spectra, sems):
+def start_reads(blocks_hbm, raw_hbm, owner_hbm, table_hbm, blocks, raw, owner, table, sems):
     copies = [
         pltpu.make_async_copy(owner_hbm, owner, sems.at[0]),
         pltpu.make_async_copy(blocks_hbm, blocks, sems.at[1]),
@@ -81,7 +81,10 @@
         )
     for copy in copies:
         copy.start()
-    zh = lax.axis_index("recv") % 4
+    return copies
+
+
+def prepare(copies, zh, blocks, raw, owner, table, slots, first, spectra):
     row = lax.broadcasted_iota(jnp.int32, (64, 512), 0)
     lane = lax.broadcasted_iota(jnp.int32, (64, 512), 1)
     diagonal = row[:, :64] == lane[:, :64]
@@ -109,45 +112,22 @@
     @pl.loop(0, 4, unroll=2)
     def _(part):
         placed = lax.broadcasted_iota(jnp.int32, (256, 512), 0) + part * 256 == target
-        slots[pl.ds(pl.multiple_of(part * 256, 256), 256), :] = product(
+        slots[pl.ds(part * 4, 4)] = product(
             placed.astype(jnp.float32).astype(jnp.bfloat16), spectra[...]
-        ).astype(jnp.bfloat16)
+        ).astype(jnp.bfloat16).reshape(4, 4, 16, WIN)
 
     for b in range(2):
         block = blocks[b]
-        start = (block // 4 * 4 + place_of((block % 4 + 4 - zh) % 4)) * 16
-        chunk[b * 16 : b * 16 + 16, :] = slots[pl.ds(pl.multiple_of(start, 16), 16), :]
-
-
-def prepare(raw_data, row_owner, source_blocks):
-    hbm = pl.BlockSpec(memory_space=pltpu.HBM)
-    vmem = pl.BlockSpec(memory_space=pltpu.VMEM)
-    return pl.pallas_call(
-        prepare_kernel,
-        out_shape=(
-            jax.ShapeDtypeStruct((1024, WIN), jnp.bfloat16),
-            jax.ShapeDtypeStruct((32, WIN), jnp.bfloat16),
-        ),
-        in_specs=[hbm] * 4,
-        out_specs=(vmem, vmem),
-        scratch_shapes=[
-            pltpu.SMEM((2,), jnp.int32),
-            pltpu.VMEM(raw_data.shape, jnp.float32),
-            pltpu.VMEM((1, 64), jnp.int32),
-            pltpu.VMEM((2, WIN, WIN), jnp.bfloat16),
-            pltpu.VMEM((512, WIN), jnp.bfloat16),
-            pltpu.SemaphoreType.DMA((8,)),
-        ],
-        compiler_params=pltpu.CompilerParams(vmem_limit_bytes=60 * 1024 * 1024),
-        name="prepare",
-    )(source_blocks, raw_data, row_owner.reshape(1, 64), forward_halves())
+        first[b * 16 : b * 16 + 16, :] = slots[block // 4, place_of((block % 4 + 4 - zh) % 4)]
 
 
 MESH = pl.DeviceIdType.MESH
 
 
-def exchange_kernel(slots, first, sources, receivers, held, panels, placed, turned, staged, chunk, turn_send, turn_recv, xy_send, xy_recv, z_send, z_recv, pair_send, pair_recv,
+def exchange_kernel(blocks_hbm, raw_hbm, owner_hbm, table_hbm, sources, receivers, blocks, raw, owner, table,
+                    spectra, read_sem, slots, first, held, panels, placed, turned, staged, chunk, turn_send, turn_recv, xy_send, xy_recv, z_send, z_recv, pair_send, pair_recv,
                     core_send, core_recv, pz_send, pz_recv, pxy_send, pxy_recv, local_sem):
+    reads = start_reads(blocks_hbm, raw_hbm, owner_hbm, table_hbm, blocks, raw, owner, table, read_sem)
     recv = lax.axis_index("recv")
     seg = lax.axis_index("seg")
     y, x, zh = recv // 16, (recv // 4) % 4, recv % 4
@@ -285,7 +265,7 @@
             & (column % 128 == channel % 32 // 2 * 8 + channel // 32 * 2 + channel % 2)
         )
 
-        @pl.loop(0, 16, unroll=2)
+        @pl.loop(0, 16, unroll=4)
         def _(n):
             for c in range(2):
                 block = placed[pl.ds(pl.multiple_of(n * 256, 256), 256), c * HALF : c * HALF + HALF]
@@ -346,6 +326,7 @@
         )
 
     pl.semaphore_signal(barrier, inc=1, device_id=(recv, zl * 2 + 1 - core), device_id_type=MESH)
+    prepare(reads, zh, blocks, raw, owner, table, slots, first, spectra)
     kept_chunk = pltpu.make_async_copy(first, chunk, local_sem.at[6])
     own_chunk = pltpu.make_async_copy(chunk, panels.at[plane, zh], local_sem.at[4])
 
@@ -463,40 +444,48 @@
             pair_copy(turn, low, half).wait_send()
 
 
-def exchange(slots, chunk):
+def exchange(raw_data, row_owner, source_blocks):
     dma = pltpu.SemaphoreType.DMA
-    rows, width = slots.shape[-2:]
+    bf16 = jnp.bfloat16
     return pl.pallas_call(
         exchange_kernel,
         out_shape=(
             jax.ShapeDtypeStruct((HALF * STEP, 128), jnp.float32),
             jax.ShapeDtypeStruct((HALF * STEP, 128), jnp.float32),
         ),
-        in_specs=[pl.BlockSpec(memory_space=pltpu.VMEM)] * 2,
+        in_specs=[pl.BlockSpec(memory_space=pltpu.HBM)] * 4,
         out_specs=(pl.BlockSpec(memory_space=pltpu.VMEM),) * 2,
         scratch_shapes=[
-            pltpu.VMEM((4, 16, 4, rows, width), jnp.bfloat16),
-            pltpu.VMEM((16, 4) + chunk.shape, jnp.bfloat16),
-            pltpu.VMEM((4096, width), jnp.bfloat16),
-            pltpu.VMEM((1024, width), jnp.bfloat16),
-            pltpu.VMEM((4, 16, rows, width), jnp.bfloat16),
-            pltpu.VMEM(chunk.shape, jnp.bfloat16),
+            pltpu.SMEM((2,), jnp.int32),
+            pltpu.VMEM(raw_data.shape, jnp.float32),
+            pltpu.VMEM((1, 64), jnp.int32),
+            pltpu.VMEM((2, WIN, WIN), bf16),
+            pltpu.VMEM((512, WIN), bf16),
+            dma((8,)),
+            pltpu.VMEM((16, 4, 16, WIN), bf16),
+            pltpu.VMEM((32, WIN), bf16),
+            pltpu.VMEM((4, 16, 4, 16, WIN), bf16),
+            pltpu.VMEM((16, 4, 32, WIN), bf16),
+            pltpu.VMEM((4096, WIN), bf16),
+            pltpu.VMEM((1024, WIN), bf16),
+            pltpu.VMEM((4, 16, 16, WIN), bf16),
+            pltpu.VMEM((32, WIN), bf16),
             dma, dma, dma((4, 16)), dma((4, 16)), dma((4, 2)), dma((4, 2, 2)),
             dma((4, 2, 2)), dma((4, 2, 2)), dma((4, 2, 2)), dma((4, 2, 2)),
             dma((4,)), dma((4,)), dma((16,)), dma((16,)), dma((7,)),
         ],
         compiler_params=pltpu.CompilerParams(
-            collective_id=0, has_side_effects=True, vmem_limit_bytes=22 * 1024 * 1024
+            collective_id=0, has_side_effects=True, vmem_limit_bytes=24576 * 1024
         ),
         name="exchange",
-    )(slots, chunk)
+    )(source_blocks, raw_data, row_owner.reshape(1, 64), forward_halves())
 
 
 def correlate_kernel(sources, receivers, inverse_hbm, out, stack, lagged, inverse, sent):
     table_copy = pltpu.make_async_copy(inverse_hbm, inverse, sent.at[2])
     table_copy.start()
 
-    @pl.loop(0, HALF, unroll=8)
+    @pl.loop(0, HALF, unroll=32)
     def _(j):
         at = pl.ds(pl.multiple_of(j * STEP, 8), 64)
         terms = lax.dot_general(
@@ -522,7 +511,7 @@
             def _():
                 out_copy(group - 2, slot).wait()
 
-            @pl.loop(0, 8, unroll=4)
+            @pl.loop(0, 8, unroll=8)
             def _(i):
                 start = (group * 8 + i) * PITCH
                 lagged[slot, i] = lax.dot_general(
@@ -556,8 +545,7 @@
 
 
 def local(raw_data, row_owner, source_blocks):
-    slots, chunk = prepare(raw_data, row_owner, source_blocks)
-    sources, receivers = exchange(slots.reshape(16, 4, 16, WIN), chunk)
+    sources, receivers = exchange(raw_data, row_owner, source_blocks)
     inverse = jnp.asarray(inverse_table(32), jnp.bfloat16)
     lagged = correlate(sources, receivers, inverse)
     return lagged.reshape(2, 32, 128, WIN)

time: 90.1 us -> 81 us (0.90)
  Pallas kernels: 86.2 us -> 74.6 us
  local copies, waits for them, and re-layouts: 3.01 us -> 4.8 us
    pallas_call x1 -> x0, Pallas kernels: 5.8 us -> none  [prepare(): pl.pallas_call(prepare_kernel, out_shape=(jax.ShapeDtypeStruct((1024, WIN...]
    pallas_call x1, Pallas kernels: 17.3 us -> 12.1 us  [correlate(): pl.pallas_call(correlate_kernel, out_shape=jax.ShapeDtypeStruct((64, 128,...]
    unnamed x6 -> x10, local copies, waits for them, and re-layouts: 3.01 us -> 4.8 us
where the time goes in v4:
time: 81 us; the launch traced here: 79.4 us
  Pallas kernels  74.6 us (92%)
  local copies, waits for them, and re-layouts  4.8 us (6%)
    pallas_call x1, Pallas kernels, exchange(): pl.pallas_call(exchange_kernel, out_shape=(jax.ShapeDtypeStruct((HALF * S...  62.5 us
    pallas_call x1, Pallas kernels, correlate(): pl.pallas_call(correlate_kernel, out_shape=jax.ShapeDtypeStruct((64, 128,...  12.1 us
    unnamed x10, local copies, waits for them, and re-layouts  4.8 us

profile of v4, /device:TPU:1, one launch (start us, length us, event | category | flops | bytes accessed | tf_op | source)
XLA Modules:
  0.0 79.4 jit_solution(12458436832541222238)
XLA Ops:
  0.0 0.0 copy-start
  0.0 1.2 %copy-done = f32[2,64,2048]{2,1,0:T(8,128)S(1)} copy-done((f32[2,64,2048]{2,1,0:T(8,128)S(1)}, f32[2,64,2048]{2,1,0:T(8,128)}, u32[]{:S(2)}) %copy-start) | copy-done | bytes 1048600
  1.2 0.0 copy-start.1
  1.2 1.2 %copy-done.1 = bf16[2,512,512]{2,1,0:T(8,128)(2,1)S(1)} copy-done((bf16[2,512,512]{2,1,0:T(8,128)(2,1)S(1)}, bf16[2,512,512]{2,1,0:T(8,128)(2,1)}, u32[]{:S(2)}) %copy-start.1) | copy-done | bytes 1048600
  2.5 0.0 copy-start.3
  2.5 0.7 copy-done.3
  3.1 0.0 copy-start.4
  3.1 0.7 copy-done.4
  3.8 62.5 %exchange.1 = (f32[18432,128]{1,0:T(8,128)S(1)}, f32[18432,128]{1,0:T(8,128)S(1)}) custom-call(s32[2]{0:T(128)S(1)} %copy-done.3, f32[2,64,2048]{2,1,0:T(8,128)S(1)} %copy-done, s32[1,64]{1,0:T(1,128)S(1)} %bitcast.2, bf16[2,512,512]{2,1,0:T(8,128)(2,1)S(1)} %copy-done.1), custom_call_target="tpu_custom_call" | custom-call | tf_op jit(solution)/shard_map/exchange/pallas_call | solution.py:450
  66.3 0.0 copy-start.2
  66.3 1.0 %copy-done.2 = bf16[512,512]{1,0:T(8,128)(2,1)S(1)} copy-done((bf16[512,512]{1,0:T(8,128)(2,1)S(1)}, bf16[512,512]{1,0:T(8,128)(2,1)}, u32[]{:S(2)}) %copy-start.2) | copy-done | bytes 524312
  67.3 12.1 %correlate.1 = bf16[64,128,512]{2,1,0:T(8,128)(2,1)} custom-call(f32[18432,128]{1,0:T(8,128)S(1)} %get-tuple-element.7.sources, f32[18432,128]{1,0:T(8,128)S(1)} %get-tuple-element.8.receivers, bf16[512,512]{1,0:T(8,128)(2,1)S(1)} %copy-done.2), custom_call_target="tpu_custom_call" | custom-call | tf_op jit(solution)/shard_map/correlate/pallas_call | solution.py:531
Async XLA Ops:
  0.0 1.2 %copy-start = (f32[2,64,2048]{2,1,0:T(8,128)S(1)}, f32[2,64,2048]{2,1,0:T(8,128)}, u32[]{:S(2)}) copy-start(f32[2,64,2048]{2,1,0:T(8,128)} %raw_hbm.1) | copy-start | bytes 3145732
  1.2 1.2 %copy-start.1 = (bf16[2,512,512]{2,1,0:T(8,128)(2,1)S(1)}, bf16[2,512,512]{2,1,0:T(8,128)(2,1)}, u32[]{:S(2)}) copy-start(bf16[2,512,512]{2,1,0:T(8,128)(2,1)} %constant.4.clone.table_hbm) | copy-start | bytes 3145732
  2.5 0.7 copy-start.3
  3.1 0.7 copy-start.4
  66.3 1.0 %copy-start.2 = (bf16[512,512]{1,0:T(8,128)(2,1)S(1)}, bf16[512,512]{1,0:T(8,128)(2,1)}, u32[]{:S(2)}) copy-start(bf16[512,512]{1,0:T(8,128)(2,1)} %constant.5.clone.inverse_hbm) | copy-start | bytes 1572868

commit v5 on v4

--- a/solution.py
+++ b/solution.py
@@ -65,38 +65,16 @@
     return place
 
 
-def start_reads(blocks_hbm, raw_hbm, owner_hbm, table_hbm, blocks, raw, owner, table, sems):
-    copies = [
-        pltpu.make_async_copy(owner_hbm, owner, sems.at[0]),
-        pltpu.make_async_copy(blocks_hbm, blocks, sems.at[1]),
-        pltpu.make_async_copy(table_hbm.at[0], table.at[0], sems.at[2]),
-        pltpu.make_async_copy(table_hbm.at[1], table.at[1], sems.at[3]),
-    ]
-    for piece in range(4):
-        rows = pl.ds(piece % 2 * 32, 32)
-        copies.append(
-            pltpu.make_async_copy(
-                raw_hbm.at[piece // 2, rows], raw.at[piece // 2, rows], sems.at[4 + piece]
-            )
-        )
-    for copy in copies:
-        copy.start()
-    return copies
-
-
-def prepare(copies, zh, blocks, raw, owner, table, slots, first, spectra):
+def prepare(zh, blocks, raw, owner, table, slots, first, spectra):
     row = lax.broadcasted_iota(jnp.int32, (64, 512), 0)
     lane = lax.broadcasted_iota(jnp.int32, (64, 512), 1)
     diagonal = row[:, :64] == lane[:, :64]
-    copies[0].wait()
     owner_column = jnp.sum(jnp.where(diagonal, owner[...], 0), axis=1, keepdims=True)
     owner_row = jnp.sum(jnp.where(row == lane % 64, owner_column, 0), axis=0, keepdims=True)
     same = (owner_column == owner_row) & (row < lane % 64)
     rank = jnp.sum(same.astype(jnp.int32), axis=0, keepdims=True)
     place = owner_row // 4 * 4 + place_of((owner_row % 4 + 4 - zh) % 4)
     target = (place * 2 + rank) * 8 + lax.broadcasted_iota(jnp.int32, (1, 512), 1) // 64
-    for copy in copies[1:]:
-        copy.wait()
     for window in range(8):
         parts = []
         for run in range(4):
@@ -124,10 +102,8 @@
 MESH = pl.DeviceIdType.MESH
 
 
-def exchange_kernel(blocks_hbm, raw_hbm, owner_hbm, table_hbm, sources, receivers, blocks, raw, owner, table,
-                    spectra, read_sem, slots, first, held, panels, placed, turned, staged, chunk, turn_send, turn_recv, xy_send, xy_recv, z_send, z_recv, pair_send, pair_recv,
+def exchange_kernel(blocks, raw, owner, table, sources, receivers, spectra, slots, first, held, panels, placed, turned, staged, chunk, turn_send, turn_recv, xy_send, xy_recv, z_send, z_recv, pair_send, pair_recv,
                     core_send, core_recv, pz_send, pz_recv, pxy_send, pxy_recv, local_sem):
-    reads = start_reads(blocks_hbm, raw_hbm, owner_hbm, table_hbm, blocks, raw, owner, table, read_sem)
     recv = lax.axis_index("recv")
     seg = lax.axis_index("seg")
     y, x, zh = recv // 16, (recv // 4) % 4, recv % 4
@@ -326,7 +302,7 @@
         )
 
     pl.semaphore_signal(barrier, inc=1, device_id=(recv, zl * 2 + 1 - core), device_id_type=MESH)
-    prepare(reads, zh, blocks, raw, owner, table, slots, first, spectra)
+    prepare(zh, blocks, raw, owner, table, slots, first, spectra)
     kept_chunk = pltpu.make_async_copy(first, chunk, local_sem.at[6])
     own_chunk = pltpu.make_async_copy(chunk, panels.at[plane, zh], local_sem.at[4])
 
@@ -453,15 +429,10 @@
             jax.ShapeDtypeStruct((HALF * STEP, 128), jnp.float32),
             jax.ShapeDtypeStruct((HALF * STEP, 128), jnp.float32),
         ),
-        in_specs=[pl.BlockSpec(memory_space=pltpu.HBM)] * 4,
+        in_specs=[pl.BlockSpec(memory_space=pltpu.SMEM)] + [pl.BlockSpec(memory_space=pltpu.VMEM)] * 3,
         out_specs=(pl.BlockSpec(memory_space=pltpu.VMEM),) * 2,
         scratch_shapes=[
-            pltpu.SMEM((2,), jnp.int32),
-            pltpu.VMEM(raw_data.shape, jnp.float32),
-            pltpu.VMEM((1, 64), jnp.int32),
-            pltpu.VMEM((2, WIN, WIN), bf16),
             pltpu.VMEM((512, WIN), bf16),
-            dma((8,)),
             pltpu.VMEM((16, 4, 16, WIN), bf16),
             pltpu.VMEM((32, WIN), bf16),
             pltpu.VMEM((4, 16, 4, 16, WIN), bf16),
@@ -485,7 +456,7 @@
     table_copy = pltpu.make_async_copy(inverse_hbm, inverse, sent.at[2])
     table_copy.start()
 
-    @pl.loop(0, HALF, unroll=32)
+    @pl.loop(0, HALF, unroll=64)
     def _(j):
         at = pl.ds(pl.multiple_of(j * STEP, 8), 64)
         terms = lax.dot_general(

time: 81 us -> 80.6 us (level)
  the two profiles are of different devices: /device:TPU:1 before, /device:TPU:25 now
where the time goes in v5:
time: 80.6 us; the launch traced here: 80.3 us
  Pallas kernels  75.5 us (94%)
  local copies, waits for them, and re-layouts  4.8 us (6%)
    pallas_call x1, Pallas kernels, exchange(): pl.pallas_call(exchange_kernel, out_shape=(jax.ShapeDtypeStruct((HALF * S...  64.2 us
    pallas_call x1, Pallas kernels, correlate(): pl.pallas_call(correlate_kernel, out_shape=jax.ShapeDtypeStruct((64, 128,...  11.3 us
    unnamed x10, local copies, waits for them, and re-layouts  4.8 us

profile of v5, /device:TPU:25, one launch (start us, length us, event | category | flops | bytes accessed | tf_op | source)
XLA Modules:
  0.0 80.3 jit_solution(17243418855559564061)
XLA Ops:
  0.0 0.0 copy-start
  0.0 1.2 %copy-done = f32[2,64,2048]{2,1,0:T(8,128)S(1)} copy-done((f32[2,64,2048]{2,1,0:T(8,128)S(1)}, f32[2,64,2048]{2,1,0:T(8,128)}, u32[]{:S(2)}) %copy-start) | copy-done | bytes 1048600
  1.2 0.0 copy-start.1
  1.2 1.2 %copy-done.1 = bf16[2,512,512]{2,1,0:T(8,128)(2,1)S(1)} copy-done((bf16[2,512,512]{2,1,0:T(8,128)(2,1)S(1)}, bf16[2,512,512]{2,1,0:T(8,128)(2,1)}, u32[]{:S(2)}) %copy-start.1) | copy-done | bytes 1048600
  2.5 0.0 copy-start.3
  2.5 0.7 copy-done.3
  3.1 0.0 copy-start.4
  3.1 0.7 copy-done.4
  3.8 64.2 %exchange.1 = (f32[18432,128]{1,0:T(8,128)S(1)}, f32[18432,128]{1,0:T(8,128)S(1)}) custom-call(s32[2]{0:T(128)S(1)} %copy-done.3, f32[2,64,2048]{2,1,0:T(8,128)S(1)} %copy-done, s32[1,64]{1,0:T(1,128)S(1)} %bitcast.2, bf16[2,512,512]{2,1,0:T(8,128)(2,1)S(1)} %copy-done.1), custom_call_target="tpu_custom_call" | custom-call | tf_op jit(solution)/shard_map/exchange/pallas_call | solution.py:426
  68.0 0.0 copy-start.2
  68.0 1.0 %copy-done.2 = bf16[512,512]{1,0:T(8,128)(2,1)S(1)} copy-done((bf16[512,512]{1,0:T(8,128)(2,1)S(1)}, bf16[512,512]{1,0:T(8,128)(2,1)}, u32[]{:S(2)}) %copy-start.2) | copy-done | bytes 524312
  69.0 11.3 %correlate.1 = bf16[64,128,512]{2,1,0:T(8,128)(2,1)} custom-call(f32[18432,128]{1,0:T(8,128)S(1)} %get-tuple-element.7.sources, f32[18432,128]{1,0:T(8,128)S(1)} %get-tuple-element.8.receivers, bf16[512,512]{1,0:T(8,128)(2,1)S(1)} %copy-done.2), custom_call_target="tpu_custom_call" | custom-call | tf_op jit(solution)/shard_map/correlate/pallas_call | solution.py:502
Async XLA Ops:
  0.0 1.2 %copy-start = (f32[2,64,2048]{2,1,0:T(8,128)S(1)}, f32[2,64,2048]{2,1,0:T(8,128)}, u32[]{:S(2)}) copy-start(f32[2,64,2048]{2,1,0:T(8,128)} %raw.1) | copy-start | bytes 3145732
  1.2 1.2 %copy-start.1 = (bf16[2,512,512]{2,1,0:T(8,128)(2,1)S(1)}, bf16[2,512,512]{2,1,0:T(8,128)(2,1)}, u32[]{:S(2)}) copy-start(bf16[2,512,512]{2,1,0:T(8,128)(2,1)} %constant.4.clone.table) | copy-start | bytes 3145732
  2.5 0.7 copy-start.3
  3.1 0.7 copy-start.4
  68.0 1.0 %copy-start.2 = (bf16[512,512]{1,0:T(8,128)(2,1)S(1)}, bf16[512,512]{1,0:T(8,128)(2,1)}, u32[]{:S(2)}) copy-start(bf16[512,512]{1,0:T(8,128)(2,1)} %constant.5.clone.inverse_hbm) | copy-start | bytes 1572868

commit v6 on v5

--- a/solution.py
+++ b/solution.py
@@ -25,17 +25,6 @@
     parity = np.where(sample % 2 == 0, 1.0, -1.0)
     sines = np.where(freq[None, :] == 0, parity[:, None], -np.sin(angles))
     return np.concatenate([np.cos(angles), sines], axis=1)
-
-
-def inverse_table(window_total):
-    lag, freq = np.arange(WIN) - HALF, np.arange(HALF)
-    angles = (freq[:, None] * lag[None, :] % WIN) * (2.0 * math.pi / WIN)
-    factor = 1.0 / (WIN * math.sqrt(window_total * WIN))
-    parity = np.where(lag % 2 == 0, 1.0, -1.0)
-    zero = freq[:, None] == 0
-    cosine_rows = np.where(zero, factor, 2.0 * factor * np.cos(angles))
-    sine_rows = np.where(zero, factor * parity[None, :], -2.0 * factor * np.sin(angles))
-    return np.concatenate([cosine_rows, sine_rows], axis=0)
 
 
 def forward_halves():
@@ -102,7 +91,7 @@
 MESH = pl.DeviceIdType.MESH
 
 
-def exchange_kernel(blocks, raw, owner, table, sources, receivers, spectra, slots, first, held, panels, placed, turned, staged, chunk, turn_send, turn_recv, xy_send, xy_recv, z_send, z_recv, pair_send, pair_recv,
+def exchange_kernel(blocks, raw, owner, table, sources, receivers, inverse, spectra, slots, first, held, panels, placed, turned, staged, chunk, turn_send, turn_recv, xy_send, xy_recv, z_send, z_recv, pair_send, pair_recv,
                     core_send, core_recv, pz_send, pz_recv, pxy_send, pxy_recv, local_sem):
     recv = lax.axis_index("recv")
     seg = lax.axis_index("seg")
@@ -250,6 +239,22 @@
                     receivers[pl.ds(c * 32 + n * 2 + w, HALF, stride=STEP), :] = part[
                         :, w * 128 : w * 128 + 128
                     ]
+
+    def turn_table():
+        same = zero_one(row == column)
+        scale = 1.0 / (WIN * math.sqrt(32 * WIN))
+        factor = jnp.where(row == 0, scale, 2.0 * scale * (1 - 2 * (row % 2)).astype(jnp.float32))
+        for c in range(2):
+            for d in range(2):
+                part = lax.dot_general(
+                    same,
+                    table[0, d * HALF : d * HALF + HALF, c * HALF : c * HALF + HALF],
+                    NT,
+                    preferred_element_type=jnp.float32,
+                )
+                inverse[c * HALF : c * HALF + HALF, d * HALF : d * HALF + HALF] = (
+                    part * factor
+                ).astype(jnp.bfloat16)
 
     def turn_sources(window_group):
         order = zero_one(row % 16 // 2 * 32 + row % 32 // 16 * 16 + row % 2 * 8 + row // 32 == column)
@@ -384,6 +389,8 @@
             core_arrival(turn, low, half).wait_recv()
         place_block(low * 2 + 1 - core, (zh + 4 - turn) % 4)
 
+    turn_table()
+
     @pl.loop(1, 16)
     def _(step):
         pxy_copy(step).wait_recv()
@@ -428,9 +435,10 @@
         out_shape=(
             jax.ShapeDtypeStruct((HALF * STEP, 128), jnp.float32),
             jax.ShapeDtypeStruct((HALF * STEP, 128), jnp.float32),
+            jax.ShapeDtypeStruct((WIN, WIN), jnp.bfloat16),
         ),
         in_specs=[pl.BlockSpec(memory_space=pltpu.SMEM)] + [pl.BlockSpec(memory_space=pltpu.VMEM)] * 3,
-        out_specs=(pl.BlockSpec(memory_space=pltpu.VMEM),) * 2,
+        out_specs=(pl.BlockSpec(memory_space=pltpu.VMEM),) * 3,
         scratch_shapes=[
             pltpu.VMEM((512, WIN), bf16),
             pltpu.VMEM((16, 4, 16, WIN), bf16),
@@ -452,10 +460,7 @@
     )(source_blocks, raw_data, row_owner.reshape(1, 64), forward_halves())
 
 
-def correlate_kernel(sources, receivers, inverse_hbm, out, stack, lagged, inverse, sent):
-    table_copy = pltpu.make_async_copy(inverse_hbm, inverse, sent.at[2])
-    table_copy.start()
-
+def correlate_kernel(sources, receivers, inverse, out, stack, lagged, sent):
     @pl.loop(0, HALF, unroll=64)
     def _(j):
         at = pl.ds(pl.multiple_of(j * STEP, 8), 64)
@@ -470,8 +475,6 @@
 
     def out_copy(group, slot):
         return pltpu.make_async_copy(lagged.at[slot], out.at[pl.ds(group * 8, 8)], sent.at[slot])
-
-    table_copy.wait()
 
     @pl.loop(0, 4)
     def _(pair):
@@ -502,13 +505,12 @@
     return pl.pallas_call(
         correlate_kernel,
         out_shape=jax.ShapeDtypeStruct((64, 128, WIN), jnp.bfloat16),
-        in_specs=[pl.BlockSpec(memory_space=pltpu.VMEM)] * 2 + [pl.BlockSpec(memory_space=pltpu.HBM)],
+        in_specs=[pl.BlockSpec(memory_space=pltpu.VMEM)] * 3,
         out_specs=pl.BlockSpec(memory_space=pl.ANY),
         scratch_shapes=[
             pltpu.VMEM((64 * PITCH, 128), jnp.float32),
             pltpu.VMEM((2, 8, 128, WIN), jnp.bfloat16),
-            pltpu.VMEM((WIN, WIN), jnp.bfloat16),
-            pltpu.SemaphoreType.DMA((3,)),
+            pltpu.SemaphoreType.DMA((2,)),
         ],
         compiler_params=pltpu.CompilerParams(vmem_limit_bytes=24 * 1024 * 1024),
         name="correlate",
@@ -516,8 +518,7 @@
 
 
 def local(raw_data, row_owner, source_blocks):
-    sources, receivers = exchange(raw_data, row_owner, source_blocks)
-    inverse = jnp.asarray(inverse_table(32), jnp.bfloat16)
+    sources, receivers, inverse = exchange(raw_data, row_owner, source_blocks)
     lagged = correlate(sources, receivers, inverse)
     return lagged.reshape(2, 32, 128, WIN)
 

time: 80.6 us -> 79.4 us (0.985)
  the two profiles are of different devices: /device:TPU:25 before, /device:TPU:1 now
where the time goes in v6:
time: 79.4 us; the launch traced here: 77.9 us
  Pallas kernels  74.1 us (93%)
  local copies, waits for them, and re-layouts  3.76 us (5%)
    pallas_call x1, Pallas kernels, exchange(): pl.pallas_call(exchange_kernel, out_shape=(jax.ShapeDtypeStruct((HALF * S...  62.8 us
    pallas_call x1, Pallas kernels, correlate(): pl.pallas_call(correlate_kernel, out_shape=jax.ShapeDtypeStruct((64, 128,...  11.3 us
    unnamed x8, local copies, waits for them, and re-layouts  3.76 us

profile of v6, /device:TPU:1, one launch (start us, length us, event | category | flops | bytes accessed | tf_op | source)
XLA Modules:
  0.0 77.9 jit_solution(18074889858983352240)
XLA Ops:
  0.0 0.0 copy-start
  0.0 1.2 %copy-done = f32[2,64,2048]{2,1,0:T(8,128)S(1)} copy-done((f32[2,64,2048]{2,1,0:T(8,128)S(1)}, f32[2,64,2048]{2,1,0:T(8,128)}, u32[]{:S(2)}) %copy-start) | copy-done | bytes 1048600
  1.2 0.0 copy-start.1
  1.2 1.2 %copy-done.1 = bf16[2,512,512]{2,1,0:T(8,128)(2,1)S(1)} copy-done((bf16[2,512,512]{2,1,0:T(8,128)(2,1)S(1)}, bf16[2,512,512]{2,1,0:T(8,128)(2,1)}, u32[]{:S(2)}) %copy-start.1) | copy-done | bytes 1048600
  2.5 0.0 copy-start.2
  2.5 0.7 copy-done.2
  3.1 0.0 copy-start.3
  3.1 0.7 copy-done.3
  3.8 62.8 %exchange.1 = (f32[18432,128]{1,0:T(8,128)S(1)}, f32[18432,128]{1,0:T(8,128)S(1)}, bf16[512,512]{1,0:T(8,128)(2,1)S(1)}) custom-call(s32[2]{0:T(128)S(1)} %copy-done.2, f32[2,64,2048]{2,1,0:T(8,128)S(1)} %copy-done, s32[1,64]{1,0:T(1,128)S(1)} %bitcast.2, bf16[2,512,512]{2,1,0:T(8,128)(2,1)S(1)} %copy-done.1), custom_call_target="tpu_custom_call" | custom-call | tf_op jit(solution)/shard_map/exchange/pallas_call | solution.py:433
  66.6 11.3 %correlate.1 = bf16[64,128,512]{2,1,0:T(8,128)(2,1)} custom-call(f32[18432,128]{1,0:T(8,128)S(1)} %get-tuple-element.8.sources, f32[18432,128]{1,0:T(8,128)S(1)} %get-tuple-element.9.receivers, bf16[512,512]{1,0:T(8,128)(2,1)S(1)} %get-tuple-element.10.inverse), custom_call_target="tpu_custom_call" | custom-call | tf_op jit(solution)/shard_map/correlate/pallas_call | solution.py:505
Async XLA Ops:
  0.0 1.2 %copy-start = (f32[2,64,2048]{2,1,0:T(8,128)S(1)}, f32[2,64,2048]{2,1,0:T(8,128)}, u32[]{:S(2)}) copy-start(f32[2,64,2048]{2,1,0:T(8,128)} %raw.1) | copy-start | bytes 3145732
  1.2 1.2 %copy-start.1 = (bf16[2,512,512]{2,1,0:T(8,128)(2,1)S(1)}, bf16[2,512,512]{2,1,0:T(8,128)(2,1)}, u32[]{:S(2)}) copy-start(bf16[2,512,512]{2,1,0:T(8,128)(2,1)} %constant.2.clone.table) | copy-start | bytes 3145732
  2.5 0.7 copy-start.2
  3.1 0.7 copy-start.3

commit v7 on v6

--- a/solution.py
+++ b/solution.py
@@ -76,7 +76,7 @@
             product(high, table[0]) + (product(low, table[0]) + product(high, table[1]))
         ).astype(jnp.bfloat16)
 
-    @pl.loop(0, 4, unroll=2)
+    @pl.loop(0, 4, unroll=4)
     def _(part):
         placed = lax.broadcasted_iota(jnp.int32, (256, 512), 0) + part * 256 == target
         slots[pl.ds(part * 4, 4)] = product(
@@ -230,7 +230,7 @@
             & (column % 128 == channel % 32 // 2 * 8 + channel // 32 * 2 + channel % 2)
         )
 
-        @pl.loop(0, 16, unroll=4)
+        @pl.loop(0, 16, unroll=8)
         def _(n):
             for c in range(2):
                 block = placed[pl.ds(pl.multiple_of(n * 256, 256), 256), c * HALF : c * HALF + HALF]

time: 79.4 us -> 80.9 us (1.019)
  the two profiles are of different devices: /device:TPU:1 before, /device:TPU:41 now
where the time goes in v7:
time: 80.9 us; the launch traced here: 80.7 us
  Pallas kernels  77 us (95%)
  local copies, waits for them, and re-layouts  3.76 us (5%)
    pallas_call x1, Pallas kernels, exchange(): pl.pallas_call(exchange_kernel, out_shape=(jax.ShapeDtypeStruct((HALF * S...  65.7 us
    pallas_call x1, Pallas kernels, correlate(): pl.pallas_call(correlate_kernel, out_shape=jax.ShapeDtypeStruct((64, 128,...  11.3 us
    unnamed x8, local copies, waits for them, and re-layouts  3.76 us

profile of v7, /device:TPU:41, one launch (start us, length us, event | category | flops | bytes accessed | tf_op | source)
XLA Modules:
  0.0 80.7 jit_solution(17617192250761672493)
XLA Ops:
  0.0 0.0 copy-start
  0.0 1.2 %copy-done = f32[2,64,2048]{2,1,0:T(8,128)S(1)} copy-done((f32[2,64,2048]{2,1,0:T(8,128)S(1)}, f32[2,64,2048]{2,1,0:T(8,128)}, u32[]{:S(2)}) %copy-start) | copy-done | bytes 1048600
  1.2 0.0 copy-start.1
  1.2 1.2 %copy-done.1 = bf16[2,512,512]{2,1,0:T(8,128)(2,1)S(1)} copy-done((bf16[2,512,512]{2,1,0:T(8,128)(2,1)S(1)}, bf16[2,512,512]{2,1,0:T(8,128)(2,1)}, u32[]{:S(2)}) %copy-start.1) | copy-done | bytes 1048600
  2.5 0.0 copy-start.2
  2.5 0.7 copy-done.2
  3.1 0.0 copy-start.3
  3.1 0.7 copy-done.3
  3.8 65.7 %exchange.1 = (f32[18432,128]{1,0:T(8,128)S(1)}, f32[18432,128]{1,0:T(8,128)S(1)}, bf16[512,512]{1,0:T(8,128)(2,1)S(1)}) custom-call(s32[2]{0:T(128)S(1)} %copy-done.2, f32[2,64,2048]{2,1,0:T(8,128)S(1)} %copy-done, s32[1,64]{1,0:T(1,128)S(1)} %bitcast.2, bf16[2,512,512]{2,1,0:T(8,128)(2,1)S(1)} %copy-done.1), custom_call_target="tpu_custom_call" | custom-call | tf_op jit(solution)/shard_map/exchange/pallas_call | solution.py:433
  69.5 11.3 %correlate.1 = bf16[64,128,512]{2,1,0:T(8,128)(2,1)} custom-call(f32[18432,128]{1,0:T(8,128)S(1)} %get-tuple-element.8.sources, f32[18432,128]{1,0:T(8,128)S(1)} %get-tuple-element.9.receivers, bf16[512,512]{1,0:T(8,128)(2,1)S(1)} %get-tuple-element.10.inverse), custom_call_target="tpu_custom_call" | custom-call | tf_op jit(solution)/shard_map/correlate/pallas_call | solution.py:505
Async XLA Ops:
  0.0 1.2 %copy-start = (f32[2,64,2048]{2,1,0:T(8,128)S(1)}, f32[2,64,2048]{2,1,0:T(8,128)}, u32[]{:S(2)}) copy-start(f32[2,64,2048]{2,1,0:T(8,128)} %raw.1) | copy-start | bytes 3145732
  1.2 1.2 %copy-start.1 = (bf16[2,512,512]{2,1,0:T(8,128)(2,1)S(1)}, bf16[2,512,512]{2,1,0:T(8,128)(2,1)}, u32[]{:S(2)}) copy-start(bf16[2,512,512]{2,1,0:T(8,128)(2,1)} %constant.2.clone.table) | copy-start | bytes 3145732
  2.5 0.7 copy-start.2
  3.1 0.7 copy-start.3
